TPU v7x, 32 devices: a whole 2x2x4 slice. The times are simulated.
32 devices in a mesh: ctx: 16 (over z, y, x), dp: 2 (over core).
Axes of the slice: x: 2, y: 2, z: 4, core: 2. Of those that a mesh axis runs over, the one named last changes fastest.
Arguments:
- queries: bfloat16 [2, 2048, 4096], P('dp', 'ctx'), may hold values from -9 to 9
- keys: bfloat16 [2, 2048, 512], P('dp', 'ctx'), may hold values from -6 to 6
- values: bfloat16 [2, 2048, 512], P('dp', 'ctx'), may hold values from -6 to 6
- output_gradient: bfloat16 [2, 2048, 4096], P('dp', 'ctx'), may hold values from -6 to 6
- adapter_query_down: bfloat16 [2, 2048, 16], P('dp', 'ctx'), may hold values from -0.29882812 to 0.29882812
- adapter_value_down: bfloat16 [2, 2048, 16], P('dp', 'ctx'), may hold values from -0.029907227 to 0.029907227
Outputs:
- query_gradient: bfloat16 [2, 2048, 4096], P('dp', 'ctx')
- key_gradient: bfloat16 [2, 2048, 512], P('dp', 'ctx')
- value_gradient: bfloat16 [2, 2048, 512], P('dp', 'ctx')
- adapter_query_up_gradient: float32 [16, 4096], replicated
- adapter_value_up_gradient: float32 [16, 512], replicated
All inputs are finite; a program needn't handle non-finite values.
Results may differ from a plain program's by a relative error of at most 0.009.
Values may be sent and summed in bfloat16 or wider, within the bound.
A program may use at most 64 MiB of HBM per device.

v0:
```python
import jax
import jax.numpy as jnp
from jax import lax
from jax.sharding import PartitionSpec as P

QUERY_HEAD_COUNT = 32
KEY_VALUE_HEADS = 4
HEAD_WIDTH = 128
GROUP_DEVS = 4


ADAPTER_SCALE = 2.0


def passed_along(block, axis, distance):
    devices = range(lax.axis_size(axis))
    route = [((i - distance) % len(devices), i) for i in devices]
    return lax.ppermute(block, axis, route)


def head_backward(head_queries, head_grad, head_keys, head_values, allowed):
    softmax_scale = head_queries.shape[-1] ** (-0.5)
    score_matrix = (
        jnp.einsum("rtd,sd->rts", head_queries, head_keys, preferred_element_type=jnp.float32)
        * softmax_scale
    )
    score_matrix = jnp.where(allowed[None], score_matrix, -1e30)
    top = jnp.max(score_matrix, axis=-1, keepdims=True)
    raised = jnp.exp(score_matrix - top)
    probs = raised / jnp.sum(raised, axis=-1, keepdims=True)
    attention_weights = probs.astype(jnp.bfloat16)
    attended_output = jnp.einsum(
        "rts,sd->rtd", attention_weights, head_values, preferred_element_type=jnp.float32
    )
    delta = jnp.sum(head_grad.astype(jnp.float32) * attended_output, axis=-1, keepdims=True)
    score_gradient = jnp.einsum(
        "rtd,sd->rts", head_grad, head_values, preferred_element_type=jnp.float32
    )
    logit_gradient = (probs * (score_gradient - delta)).astype(jnp.bfloat16)
    query_part = (
        jnp.einsum("rts,sd->rtd", logit_gradient, head_keys, preferred_element_type=jnp.float32)
        * softmax_scale
    )
    key_part = (
        jnp.einsum("rts,rtd->sd", logit_gradient, head_queries, preferred_element_type=jnp.float32)
        * softmax_scale
    )
    value_part = jnp.einsum(
        "rts,rtd->sd", attention_weights, head_grad, preferred_element_type=jnp.float32
    )
    return (query_part.astype(jnp.bfloat16), key_part, value_part)


def attend_block(query_heads, grad_heads, key_all, value_all, places):
    rows = query_heads.shape[0]
    column = jnp.arange(key_all.shape[0])
    distance = GROUP_DEVS - 1 - column // rows
    within = column % rows
    query_row = jnp.arange(rows)

    def per_head(inputs):
        head_queries, head_grad, head_keys, head_values, place = inputs
        allowed = (distance[None, :] <= place) & (
            (distance[None, :] > 0) | (within[None, :] <= query_row[:, None])
        )
        return head_backward(head_queries, head_grad, head_keys, head_values, allowed)

    query_part, key_part, value_part = lax.map(
        per_head,
        (
            query_heads.transpose(1, 2, 0, 3),
            grad_heads.transpose(1, 2, 0, 3),
            key_all.transpose(1, 0, 2),
            value_all.transpose(1, 0, 2),
            places,
        ),
    )
    return (
        query_part.transpose(2, 0, 1, 3),
        key_part.transpose(1, 0, 2),
        value_part.transpose(1, 0, 2),
    )


def gather_keys(key_heads, value_heads):
    earlier = [
        passed_along((key_heads, value_heads), "ctx", distance) for distance in range(1, GROUP_DEVS)
    ]
    ordered = earlier[::-1] + [(key_heads, value_heads)]
    key_all = jnp.concatenate([piece[0] for piece in ordered], axis=0)
    value_all = jnp.concatenate([piece[1] for piece in ordered], axis=0)
    return (key_all, value_all)


def return_grads(terms):
    rounded = terms.astype(jnp.bfloat16)
    total = rounded[GROUP_DEVS - 1].astype(jnp.float32)
    for distance in range(1, GROUP_DEVS):
        arrived = passed_along(rounded[GROUP_DEVS - 1 - distance], "ctx", -distance)
        total = total + arrived.astype(jnp.float32)
    return total


def body(queries, keys, values, output_gradient, adapter_query_down, adapter_value_down):
    rows = queries.shape[1]
    per_head = QUERY_HEAD_COUNT // KEY_VALUE_HEADS
    half = KEY_VALUE_HEADS // 2
    query_heads = queries[0].reshape(rows, KEY_VALUE_HEADS, per_head, HEAD_WIDTH)
    grad_heads = output_gradient[0].reshape(rows, KEY_VALUE_HEADS, per_head, HEAD_WIDTH)
    key_heads = keys[0].reshape(rows, KEY_VALUE_HEADS, HEAD_WIDTH)
    value_heads = values[0].reshape(rows, KEY_VALUE_HEADS, HEAD_WIDTH)
    position = lax.axis_index("ctx")
    mine = position % GROUP_DEVS
    rolled_place = (position - GROUP_DEVS // 2) % GROUP_DEVS
    places = jnp.where(jnp.arange(KEY_VALUE_HEADS) < half, mine, rolled_place)
    key_all, value_all = gather_keys(key_heads, value_heads)
    query_part, key_part, value_part = attend_block(
        query_heads, grad_heads, key_all, value_all, places
    )
    terms = jnp.stack(
        [
            key_part.reshape(GROUP_DEVS, rows, KEY_VALUE_HEADS * HEAD_WIDTH),
            value_part.reshape(GROUP_DEVS, rows, KEY_VALUE_HEADS * HEAD_WIDTH),
        ],
        axis=1,
    )
    total = return_grads(terms).astype(jnp.bfloat16)
    query_flattened = query_part.reshape(rows, QUERY_HEAD_COUNT * HEAD_WIDTH)
    key_flattened = total[0]
    value_flattened = total[1]
    query_adapter_term = ADAPTER_SCALE * jnp.dot(
        adapter_query_down[0].T, query_flattened, preferred_element_type=jnp.float32
    )
    value_adapter_term = ADAPTER_SCALE * jnp.dot(
        adapter_value_down[0].T, value_flattened, preferred_element_type=jnp.float32
    )
    adapter_query_up_gradient, adapter_value_up_gradient = lax.psum(
        (query_adapter_term, value_adapter_term), ("ctx", "dp")
    )
    return (
        query_flattened[None],
        key_flattened[None],
        value_flattened[None],
        adapter_query_up_gradient,
        adapter_value_up_gradient,
    )


def solution(mesh):
    in_specs = (
        P("dp", "ctx", None),
        P("dp", "ctx", None),
        P("dp", "ctx", None),
        P("dp", "ctx", None),
        P("dp", "ctx", None),
        P("dp", "ctx", None),
    )
    out_specs = (P("dp", "ctx", None), P("dp", "ctx", None), P("dp", "ctx", None), P(), P())
    return jax.shard_map(body, mesh=mesh, in_specs=in_specs, out_specs=out_specs, check_vma=False)
```

profile of v0, /device:TPU:0, one launch (start us, length us, event | category | flops | bytes accessed | tf_op | source)
XLA Modules:
  0.0 247.9 jit_solution(17813957517996445667)
XLA Ops:
  7.2 1.1 copy.23
  8.3 3.9 %collective-permute-start = (bf16[128,4,128]{0,2,1:T(8,128)(2,1)S(1)}, bf16[128,4,128]{0,2,1:T(8,128)(2,1)S(1)}, u32[]{:S(2)}, u32[]{:S(2)}) collective-permute-start(bf16[128,4,128]{0,2,1:T(8,128)(2,1)S(1)} %bitcast.184), channel_id=1, source_target_pairs={{26,0},{28,2},{30,4},{0,6},{2,8},{4,10},{6,12},{8,14},{10,16},{12,... | collective-permute-start | bytes 393224 | tf_op jit(solution)/shard_map/ppermute | solution.py:18
  12.3 1.5 collective-permute-start.1
  14.4 1.0 copy.25
  15.4 3.4 %collective-permute-start.3 = (bf16[128,4,128]{0,2,1:T(8,128)(2,1)S(1)}, bf16[128,4,128]{0,2,1:T(8,128)(2,1)S(1)}, u32[]{:S(2)}, u32[]{:S(2)}) collective-permute-start(bf16[128,4,128]{0,2,1:T(8,128)(2,1)S(1)} %bitcast.180), channel_id=1, source_target_pairs={{26,0},{28,2},{30,4},{0,6},{2,8},{4,10},{6,12},{8,14},{10,16},{12,... | collective-permute-start | bytes 393224 | tf_op jit(solution)/shard_map/ppermute | solution.py:18
  18.8 1.5 collective-permute-start.4
  20.4 1.7 collective-permute-start.5
  22.1 1.6 copy.22
  24.4 1.7 collective-permute-done.2
  26.1 1.1 maximum_bitcast_fusion
  27.5 5.6 %collective-permute-done.5 = bf16[128,4,128]{0,2,1:T(8,128)(2,1)} collective-permute-done((bf16[128,4,128]{0,2,1:T(8,128)(2,1)S(1)}, bf16[128,4,128]{0,2,1:T(8,128)(2,1)}, u32[]{:S(2)}, u32[]{:S(2)}) %collective-permute-start.5) | collective-permute-done | bytes 131104 | tf_op jit(solution)/shard_map/ppermute | solution.py:18
  33.1 1.9 maximum_bitcast_fusion.1
  35.0 67.0 %while.16 = (s32[]{:T(128)}, bf16[4,8,128,128]{2,3,1,0:T(8,128)(2,1)}, bf16[4,512,128]{2,1,0:T(8,128)(2,1)}, bf16[4,512,128]{2,1,0:T(8,128)(2,1)}, s32[4]{0:T(12...) while((s32[]{:T(128)}, ...), condition=%wide.region_4.5_spmd.clone.clone, body=%wide.region_0.4_spmd.clone.clone.sunk | while | flops 1084107776 | bytes 25728236 | solution.py:68
  36.4 2.2 fusion.142
  38.8 3.0 %fusion.143 = f32[8,128]{1,0:T(8,128)S(1)} fusion(bf16[1,8,128,128]{3,2,1,0:T(8,128)(2,1)S(1)} %copy.47, bf16[4,512,128]{1,2,0:T(8,128)(2,1)} %get-tuple-element.257, s32[]{:T(128)} %get-tuple-element.239, f32[8,128]{1,0:T(8,128)S(1)} %get-tuple-element.227, pred[128,512]{1,0:T(8,128)(4,1)S(1)} %fusion.141, ...), kind=kOutput, calls=%fused_computation.11.clone.1 | convolution fusion | flops 271450624 | bytes 861696 | tf_op jit(solution)/shard_map/while/body/eval_jaxpr/rts,sd->rtd/dot_general | solution.py:32
  41.9 2.2 multiply_convert_fusion.2
  45.4 2.1 fusion.145
  47.5 3.4 %fusion.146 = bf16[4,512,128]{2,1,0:T(8,128)(2,1)S(1)} fusion(bf16[4,512,128]{2,1,0:T(8,128)(2,1)S(1)} %copy-done.5, s32[]{:T(128)} %get-tuple-element.239, bf16[4,8,128,128]{2,3,1,0:T(8,128)(2,1)S(1)} %get-tuple-element.256, f32[8,128]{1,0:T(8,128)S(1)} %get-tuple-element.227, pred[128,512]{1,0:T(8,128)(4,1)S(1)} %fusion.141, ...), kind=kOutput, calls=%fused_computation.13.clone.1 | convolution fusion | flops 271058432 | bytes 989184 | tf_op jit(solution)/shard_map/while/body/eval_jaxpr/rts,rtd->sd/dot_general | solution.py:48
  50.9 0.8 copy-done.6
  53.1 2.2 fusion.142
  55.6 3.0 %fusion.143 = f32[8,128]{1,0:T(8,128)S(1)} fusion(bf16[1,8,128,128]{3,2,1,0:T(8,128)(2,1)S(1)} %copy.47, bf16[4,512,128]{1,2,0:T(8,128)(2,1)} %get-tuple-element.257, s32[]{:T(128)} %get-tuple-element.239, f32[8,128]{1,0:T(8,128)S(1)} %get-tuple-element.227, pred[128,512]{1,0:T(8,128)(4,1)S(1)} %fusion.141, ...), kind=kOutput, calls=%fused_computation.11.clone.1 | convolution fusion | flops 271450624 | bytes 861696 | tf_op jit(solution)/shard_map/while/body/eval_jaxpr/rts,sd->rtd/dot_general | solution.py:32
  58.6 2.2 multiply_convert_fusion.2
  62.1 2.1 fusion.145
  64.2 3.4 %fusion.146 = bf16[4,512,128]{2,1,0:T(8,128)(2,1)S(1)} fusion(bf16[4,512,128]{2,1,0:T(8,128)(2,1)S(1)} %copy-done.5, s32[]{:T(128)} %get-tuple-element.239, bf16[4,8,128,128]{2,3,1,0:T(8,128)(2,1)S(1)} %get-tuple-element.256, f32[8,128]{1,0:T(8,128)S(1)} %get-tuple-element.227, pred[128,512]{1,0:T(8,128)(4,1)S(1)} %fusion.141, ...), kind=kOutput, calls=%fused_computation.13.clone.1 | convolution fusion | flops 271058432 | bytes 989184 | tf_op jit(solution)/shard_map/while/body/eval_jaxpr/rts,rtd->sd/dot_general | solution.py:48
  67.6 0.8 copy-done.6
  69.8 2.2 fusion.142
  72.3 3.0 %fusion.143 = f32[8,128]{1,0:T(8,128)S(1)} fusion(bf16[1,8,128,128]{3,2,1,0:T(8,128)(2,1)S(1)} %copy.47, bf16[4,512,128]{1,2,0:T(8,128)(2,1)} %get-tuple-element.257, s32[]{:T(128)} %get-tuple-element.239, f32[8,128]{1,0:T(8,128)S(1)} %get-tuple-element.227, pred[128,512]{1,0:T(8,128)(4,1)S(1)} %fusion.141, ...), kind=kOutput, calls=%fused_computation.11.clone.1 | convolution fusion | flops 271450624 | bytes 861696 | tf_op jit(solution)/shard_map/while/body/eval_jaxpr/rts,sd->rtd/dot_general | solution.py:32
  75.3 2.2 multiply_convert_fusion.2
  78.9 2.1 fusion.145
  81.0 3.4 %fusion.146 = bf16[4,512,128]{2,1,0:T(8,128)(2,1)S(1)} fusion(bf16[4,512,128]{2,1,0:T(8,128)(2,1)S(1)} %copy-done.5, s32[]{:T(128)} %get-tuple-element.239, bf16[4,8,128,128]{2,3,1,0:T(8,128)(2,1)S(1)} %get-tuple-element.256, f32[8,128]{1,0:T(8,128)S(1)} %get-tuple-element.227, pred[128,512]{1,0:T(8,128)(4,1)S(1)} %fusion.141, ...), kind=kOutput, calls=%fused_computation.13.clone.1 | convolution fusion | flops 271058432 | bytes 989184 | tf_op jit(solution)/shard_map/while/body/eval_jaxpr/rts,rtd->sd/dot_general | solution.py:48
  84.4 0.8 copy-done.6
  86.6 2.2 fusion.142
  89.0 3.0 %fusion.143 = f32[8,128]{1,0:T(8,128)S(1)} fusion(bf16[1,8,128,128]{3,2,1,0:T(8,128)(2,1)S(1)} %copy.47, bf16[4,512,128]{1,2,0:T(8,128)(2,1)} %get-tuple-element.257, s32[]{:T(128)} %get-tuple-element.239, f32[8,128]{1,0:T(8,128)S(1)} %get-tuple-element.227, pred[128,512]{1,0:T(8,128)(4,1)S(1)} %fusion.141, ...), kind=kOutput, calls=%fused_computation.11.clone.1 | convolution fusion | flops 271450624 | bytes 861696 | tf_op jit(solution)/shard_map/while/body/eval_jaxpr/rts,sd->rtd/dot_general | solution.py:32
  92.1 2.2 multiply_convert_fusion.2
  95.6 2.1 fusion.145
  97.7 3.4 %fusion.146 = bf16[4,512,128]{2,1,0:T(8,128)(2,1)S(1)} fusion(bf16[4,512,128]{2,1,0:T(8,128)(2,1)S(1)} %copy-done.5, s32[]{:T(128)} %get-tuple-element.239, bf16[4,8,128,128]{2,3,1,0:T(8,128)(2,1)S(1)} %get-tuple-element.256, f32[8,128]{1,0:T(8,128)S(1)} %get-tuple-element.227, pred[128,512]{1,0:T(8,128)(4,1)S(1)} %fusion.141, ...), kind=kOutput, calls=%fused_computation.13.clone.1 | convolution fusion | flops 271058432 | bytes 989184 | tf_op jit(solution)/shard_map/while/body/eval_jaxpr/rts,rtd->sd/dot_general | solution.py:48
  101.1 0.8 copy-done.6
  101.9 1.5 copy.31
  105.2 1.4 collective-permute-start.7
  106.6 1.7 collective-permute-start.8
  108.2 1.3 copy.33
  109.5 1.1 fusion.84
  110.6 3.2 %collective-permute-done.6 = bf16[2,128,512]{2,1,0:T(8,128)(2,1)S(1)} collective-permute-done((bf16[2,128,512]{2,1,0:T(8,128)(2,1)}, bf16[2,128,512]{2,1,0:T(8,128)(2,1)S(1)}, u32[]{:S(2)}, u32[]{:S(2)}) %collective-permute-start.6) | collective-permute-done | bytes 262176 | tf_op jit(solution)/shard_map/ppermute | solution.py:18
  113.8 6.3 %collective-permute-done.7 = bf16[2,128,512]{2,1,0:T(8,128)(2,1)S(1)} collective-permute-done((bf16[2,128,512]{2,1,0:T(8,128)(2,1)S(1)}, bf16[2,128,512]{2,1,0:T(8,128)(2,1)S(1)}, u32[]{:S(2)}, u32[]{:S(2)}) %collective-permute-start.7) | collective-permute-done | bytes 262176 | tf_op jit(solution)/shard_map/ppermute | solution.py:18
  120.1 4.0 %collective-permute-done.8 = bf16[2,128,512]{2,1,0:T(8,128)(2,1)S(1)} collective-permute-done((bf16[2,128,512]{2,1,0:T(8,128)(2,1)S(1)}, bf16[2,128,512]{2,1,0:T(8,128)(2,1)S(1)}, u32[]{:S(2)}, u32[]{:S(2)}) %collective-permute-start.8) | collective-permute-done | bytes 262176 | tf_op jit(solution)/shard_map/ppermute | solution.py:18
  125.1 39.8 %psum.15 = f32[16,512]{1,0:T(8,128)} all-reduce(f32[16,512]{1,0:T(8,128)S(1)} %fusion.85), channel_id=1, replica_groups=mesh['ctx'=16,'dp'=2] {'ctx','dp'}, use_global_device_ids=true, to_apply=%region_6.7 | all-reduce | flops 8192 | bytes 65536 | tf_op jit(solution)/shard_map/psum | solution.py:137
  164.9 74.5 %all-reduce.2.cloned.1.call-done = f32[16,4096]{1,0:T(8,128)} async-done(((f32[16,4096]{1,0:T(8,128)}), f32[16,4096]{1,0:T(8,128)}) %all-reduce.2.cloned.1.call-update) | async-done | bytes 262160 | tf_op jit(solution)/shard_map/psum | solution.py:137
  239.4 1.7 copy.68
  (100 shorter events, 16.0 us)
Async XLA Ops:
  7.2 102.4 %copy-start = (bf16[1,128,16]{1,2,0:T(8,128)(2,1)S(1)}, bf16[1,128,16]{1,2,0:T(8,128)(2,1)}, u32[]{:S(2)}) copy-start(bf16[1,128,16]{1,2,0:T(8,128)(2,1)} %param.12) | copy-start | bytes 12292
  7.2 16.6 %copy-start.4 = (bf16[1,128,4096]{2,1,0:T(8,128)(2,1)S(1)}, bf16[1,128,4096]{2,1,0:T(8,128)(2,1)}, u32[]{:S(2)}) copy-start(bf16[1,128,4096]{2,1,0:T(8,128)(2,1)} %param.11) | copy-start | bytes 3145732
  7.2 232.2 %all-reduce.2.cloned.1.call-start = ((), (), s32[]{:S(2)}) async-start(), calls=%async_computation | async-start | bytes 524288 | tf_op jit(solution)/shard_map/psum | solution.py:137
  8.3 12.0 %collective-permute-start = (bf16[128,4,128]{0,2,1:T(8,128)(2,1)S(1)}, bf16[128,4,128]{0,2,1:T(8,128)(2,1)S(1)}, u32[]{:S(2)}, u32[]{:S(2)}) collective-permute-start(bf16[128,4,128]{0,2,1:T(8,128)(2,1)S(1)} %bitcast.184), channel_id=1, source_target_pairs={{26,0},{28,2},{30,4},{0,6},{2,8},{4,10},{6,12},{8,14},{10,16},{12,... | collective-permute-start | bytes 393224 | tf_op jit(solution)/shard_map/ppermute | solution.py:18
  12.3 12.1 %collective-permute-start.1 = (bf16[128,4,128]{0,2,1:T(8,128)(2,1)S(1)}, bf16[128,4,128]{0,2,1:T(8,128)(2,1)}, u32[]{:S(2)}, u32[]{:S(2)}) collective-permute-start(bf16[128,4,128]{0,2,1:T(8,128)(2,1)S(1)} %bitcast.185), channel_id=1, source_target_pairs={{28,0},{30,2},{0,4},{2,6},{4,8},{6,10},{8,12},{10,14},{12,16},{14,... | collective-permute-start | bytes 393224 | tf_op jit(solution)/shard_map/ppermute | solution.py:18
  13.8 12.3 %collective-permute-start.2 = (bf16[128,4,128]{0,2,1:T(8,128)(2,1)S(1)}, bf16[128,4,128]{0,2,1:T(8,128)(2,1)}, u32[]{:S(2)}, u32[]{:S(2)}) collective-permute-start(bf16[128,4,128]{0,2,1:T(8,128)(2,1)S(1)} %bitcast.186), channel_id=1, source_target_pairs={{30,0},{0,2},{2,4},{4,6},{6,8},{8,10},{10,12},{12,14},{14,16},{16,... | collective-permute-start | bytes 393224 | tf_op jit(solution)/shard_map/ppermute | solution.py:18
  15.4 11.8 %collective-permute-start.3 = (bf16[128,4,128]{0,2,1:T(8,128)(2,1)S(1)}, bf16[128,4,128]{0,2,1:T(8,128)(2,1)S(1)}, u32[]{:S(2)}, u32[]{:S(2)}) collective-permute-start(bf16[128,4,128]{0,2,1:T(8,128)(2,1)S(1)} %bitcast.180), channel_id=1, source_target_pairs={{26,0},{28,2},{30,4},{0,6},{2,8},{4,10},{6,12},{8,14},{10,16},{12,... | collective-permute-start | bytes 393224 | tf_op jit(solution)/shard_map/ppermute | solution.py:18
  18.8 8.7 %collective-permute-start.4 = (bf16[128,4,128]{0,2,1:T(8,128)(2,1)S(1)}, bf16[128,4,128]{0,2,1:T(8,128)(2,1)}, u32[]{:S(2)}, u32[]{:S(2)}) collective-permute-start(bf16[128,4,128]{0,2,1:T(8,128)(2,1)S(1)} %bitcast.181), channel_id=1, source_target_pairs={{28,0},{30,2},{0,4},{2,6},{4,8},{6,10},{8,12},{10,14},{12,16},{14,... | collective-permute-start | bytes 393224 | tf_op jit(solution)/shard_map/ppermute | solution.py:18
  20.4 1.7 copy-start.9
  20.4 12.7 %collective-permute-start.5 = (bf16[128,4,128]{0,2,1:T(8,128)(2,1)S(1)}, bf16[128,4,128]{0,2,1:T(8,128)(2,1)}, u32[]{:S(2)}, u32[]{:S(2)}) collective-permute-start(bf16[128,4,128]{0,2,1:T(8,128)(2,1)S(1)} %bitcast.182), channel_id=1, source_target_pairs={{30,0},{0,2},{2,4},{4,6},{6,8},{8,10},{10,12},{12,14},{14,16},{16,... | collective-permute-start | bytes 393224 | tf_op jit(solution)/shard_map/ppermute | solution.py:18
  35.0 3.8 %copy-start.1 = (bf16[4,8,128,128]{2,3,1,0:T(8,128)(2,1)}, bf16[4,8,128,128]{2,3,1,0:T(8,128)(2,1)S(1)}, u32[]{:S(2)}) copy-start(bf16[4,8,128,128]{2,3,1,0:T(8,128)(2,1)S(1)} %get-tuple-element.254) | copy-start | bytes 3145732 | tf_op jit(solution)/shard_map/while
  44.7 2.8 %copy-start.5 = (bf16[4,512,128]{2,1,0:T(8,128)(2,1)S(1)}, bf16[4,512,128]{2,1,0:T(8,128)(2,1)}, u32[]{:S(2)}) copy-start(bf16[4,512,128]{2,1,0:T(8,128)(2,1)} %get-tuple-element.242) | copy-start | bytes 1572868 | tf_op jit(solution)/shard_map/while
  47.5 4.2 %copy-start.2 = (bf16[4,8,128,128]{2,3,1,0:T(8,128)(2,1)S(1)}, bf16[4,8,128,128]{2,3,1,0:T(8,128)(2,1)}, u32[]{:S(2)}) copy-start(bf16[4,8,128,128]{2,3,1,0:T(8,128)(2,1)} %copy-done.1) | copy-start | bytes 3145732 | tf_op jit(solution)/shard_map/while
  50.9 0.8 copy-start.6
  51.7 3.8 %copy-start.1 = (bf16[4,8,128,128]{2,3,1,0:T(8,128)(2,1)}, bf16[4,8,128,128]{2,3,1,0:T(8,128)(2,1)S(1)}, u32[]{:S(2)}) copy-start(bf16[4,8,128,128]{2,3,1,0:T(8,128)(2,1)S(1)} %get-tuple-element.254) | copy-start | bytes 3145732 | tf_op jit(solution)/shard_map/while
  61.4 2.8 %copy-start.5 = (bf16[4,512,128]{2,1,0:T(8,128)(2,1)S(1)}, bf16[4,512,128]{2,1,0:T(8,128)(2,1)}, u32[]{:S(2)}) copy-start(bf16[4,512,128]{2,1,0:T(8,128)(2,1)} %get-tuple-element.242) | copy-start | bytes 1572868 | tf_op jit(solution)/shard_map/while
  64.2 4.2 %copy-start.2 = (bf16[4,8,128,128]{2,3,1,0:T(8,128)(2,1)S(1)}, bf16[4,8,128,128]{2,3,1,0:T(8,128)(2,1)}, u32[]{:S(2)}) copy-start(bf16[4,8,128,128]{2,3,1,0:T(8,128)(2,1)} %copy-done.1) | copy-start | bytes 3145732 | tf_op jit(solution)/shard_map/while
  67.6 0.8 copy-start.6
  68.4 3.8 %copy-start.1 = (bf16[4,8,128,128]{2,3,1,0:T(8,128)(2,1)}, bf16[4,8,128,128]{2,3,1,0:T(8,128)(2,1)S(1)}, u32[]{:S(2)}) copy-start(bf16[4,8,128,128]{2,3,1,0:T(8,128)(2,1)S(1)} %get-tuple-element.254) | copy-start | bytes 3145732 | tf_op jit(solution)/shard_map/while
  78.1 2.9 %copy-start.5 = (bf16[4,512,128]{2,1,0:T(8,128)(2,1)S(1)}, bf16[4,512,128]{2,1,0:T(8,128)(2,1)}, u32[]{:S(2)}) copy-start(bf16[4,512,128]{2,1,0:T(8,128)(2,1)} %get-tuple-element.242) | copy-start | bytes 1572868 | tf_op jit(solution)/shard_map/while
  81.0 4.2 %copy-start.2 = (bf16[4,8,128,128]{2,3,1,0:T(8,128)(2,1)S(1)}, bf16[4,8,128,128]{2,3,1,0:T(8,128)(2,1)}, u32[]{:S(2)}) copy-start(bf16[4,8,128,128]{2,3,1,0:T(8,128)(2,1)} %copy-done.1) | copy-start | bytes 3145732 | tf_op jit(solution)/shard_map/while
  84.4 0.8 copy-start.6
  85.2 3.8 %copy-start.1 = (bf16[4,8,128,128]{2,3,1,0:T(8,128)(2,1)}, bf16[4,8,128,128]{2,3,1,0:T(8,128)(2,1)S(1)}, u32[]{:S(2)}) copy-start(bf16[4,8,128,128]{2,3,1,0:T(8,128)(2,1)S(1)} %get-tuple-element.254) | copy-start | bytes 3145732 | tf_op jit(solution)/shard_map/while
  94.9 2.8 %copy-start.5 = (bf16[4,512,128]{2,1,0:T(8,128)(2,1)S(1)}, bf16[4,512,128]{2,1,0:T(8,128)(2,1)}, u32[]{:S(2)}) copy-start(bf16[4,512,128]{2,1,0:T(8,128)(2,1)} %get-tuple-element.242) | copy-start | bytes 1572868 | tf_op jit(solution)/shard_map/while
  97.7 4.2 %copy-start.2 = (bf16[4,8,128,128]{2,3,1,0:T(8,128)(2,1)S(1)}, bf16[4,8,128,128]{2,3,1,0:T(8,128)(2,1)}, u32[]{:S(2)}) copy-start(bf16[4,8,128,128]{2,3,1,0:T(8,128)(2,1)} %copy-done.1) | copy-start | bytes 3145732 | tf_op jit(solution)/shard_map/while
  101.1 0.8 copy-start.6
  101.9 1.8 copy-start.7
  104.1 4.1 %copy-start.3 = (bf16[4,8,128,128]{2,3,1,0:T(8,128)(2,1)S(1)}, bf16[4,8,128,128]{2,3,1,0:T(8,128)(2,1)}, u32[]{:S(2)}) copy-start(bf16[4,8,128,128]{2,3,1,0:T(8,128)(2,1)} %get-tuple-element.72) | copy-start | bytes 3145732
  105.2 8.7 %collective-permute-start.6 = (bf16[2,128,512]{2,1,0:T(8,128)(2,1)}, bf16[2,128,512]{2,1,0:T(8,128)(2,1)S(1)}, u32[]{:S(2)}, u32[]{:S(2)}) collective-permute-start(bf16[2,128,512]{2,1,0:T(8,128)(2,1)} %get-tuple-element.161), channel_id=1, source_target_pairs={{2,0},{4,2},{6,4},{8,6},{10,8},{12,10},{14,12},{16,14},{18,16},{20... | collective-permute-start | bytes 786440 | tf_op jit(solution)/shard_map/ppermute | solution.py:18
  105.2 15.0 %collective-permute-start.7 = (bf16[2,128,512]{2,1,0:T(8,128)(2,1)S(1)}, bf16[2,128,512]{2,1,0:T(8,128)(2,1)S(1)}, u32[]{:S(2)}, u32[]{:S(2)}) collective-permute-start(bf16[2,128,512]{2,1,0:T(8,128)(2,1)S(1)} %get-tuple-element.163), channel_id=1, source_target_pairs={{4,0},{6,2},{8,4},{10,6},{12,8},{14,10},{16,12},{18,14},{20,16},{2... | collective-permute-start | bytes 786440 | tf_op jit(solution)/shard_map/ppermute | solution.py:18
  106.6 17.6 %collective-permute-start.8 = (bf16[2,128,512]{2,1,0:T(8,128)(2,1)S(1)}, bf16[2,128,512]{2,1,0:T(8,128)(2,1)S(1)}, u32[]{:S(2)}, u32[]{:S(2)}) collective-permute-start(bf16[2,128,512]{2,1,0:T(8,128)(2,1)S(1)} %get-tuple-element.162), channel_id=1, source_target_pairs={{6,0},{8,2},{10,4},{12,6},{14,8},{16,10},{18,12},{20,14},{22,16},{... | collective-permute-start | bytes 786440 | tf_op jit(solution)/shard_map/ppermute | solution.py:18
  109.5 15.4 %copy-start.10 = (bf16[1,128,16]{1,2,0:T(8,128)(2,1)S(1)}, bf16[1,128,16]{1,2,0:T(8,128)(2,1)}, u32[]{:S(2)}) copy-start(bf16[1,128,16]{1,2,0:T(8,128)(2,1)} %param.13) | copy-start | bytes 12292
  124.9 116.1 %copy-start.8 = (bf16[1,128,512]{2,1,0:T(8,128)(2,1)}, bf16[1,128,512]{2,1,0:T(8,128)(2,1)S(1)}, u32[]{:S(2)}) copy-start(bf16[1,128,512]{2,1,0:T(8,128)(2,1)S(1)} %get-tuple-element.261) | copy-start | bytes 393220
Sparse Core Ops, SparseCore 0:
  110.8 128.5 all-reduce.1
where the time goes:
time: 249 us; the launch traced here: 248 us
  waiting for transfers between devices  95.5 us (38%)
  matrix products  54.6 us (22%)
  blocking collectives  39.8 us (16%)
  local copies, waits for them, and re-layouts  21.6 us (9%)
  starting transfers between devices  15.8 us (6%)
  between operations  14.2 us (6%)
  other arithmetic  6 us (2%)
    psum x1, waiting for transfers between devices, body(): lax.psum((query_adapter_term, value_adapter_term), ('ctx', 'dp'))  74.5 us
    psum x1, blocking collectives, body(): lax.psum((query_adapter_term, value_adapter_term), ('ctx', 'dp'))  39.8 us
    ppermute x9, waiting for transfers between devices, passed_along(): return lax.ppermute(block, axis, route)  21 us
    ppermute x9, starting transfers between devices, passed_along(): return lax.ppermute(block, axis, route)  15.8 us
    dot_general x4, matrix products, head_backward(): jnp.einsum('rts,rtd->sd', attention_weights, head_grad, preferred_element...  13.6 us
    dot_general x4, matrix products, head_backward(): jnp.einsum('rts,sd->rtd', attention_weights, head_values, preferred_eleme...  12.2 us
    sub x4, matrix products, head_backward(): raised = jnp.exp(score_matrix - top)  8.9 us
    dot_general x4, matrix products, head_backward(): jnp.einsum('rtd,sd->rts', head_grad, head_values, preferred_element_type=...  8.63 us
  transfers between devices with their start and end apart: 10, of which 7 were waited for; matrix products, arithmetic and copies ran while one was open for 3% of the time, Pallas kernels for 0%

commit v1 on v0

v1 whole, which is shorter than its diff:
```python
import functools

import jax
import jax.numpy as jnp
from jax import lax
from jax.experimental import pallas as pl
from jax.experimental.pallas import tpu as pltpu
from jax.sharding import PartitionSpec as P

KEY_VALUE_HEADS = 4
PER_HEAD = 8
WIDTH = 128
ROWS = 128
RANK = 16
PLACES = 4
HALF_KEYS = 256
HALF_QUERIES = 2048
PLANE = 8
TILES = 5
VALUE_TILE = 2
ADAPTER_SCALE = 2.0
SCALE = WIDTH ** (-0.5)
LOG2E = 1.4426950408889634
MESH = pl.DeviceIdType.MESH
NT = (((1,), (1,)), ((), ()))
TN = (((0,), (0,)), ((), ()))
NN = (((1,), (0,)), ((), ()))


def matmul(a, b, dims):
    return lax.dot_general(a, b, dims, preferred_element_type=jnp.float32)


def kernel(
    ctx_size, dp_size,
    q_hbm, k_hbm, v_hbm, g_hbm, aq_hbm, av_hbm,
    dq_hbm, dk_out, dv_out, uq_out, uv_out,
    q_buf, g_buf, aq_buf, dq_buf, k_buf, v_buf, av_buf, w_buf, l_buf,
    part, arrived, l1_send, l1_recv, l2_recv, l3_recv,
    load_sem, own_sem, dq_sem, kv_send, kv_recv, ret_send, ret_recv,
    l1_ssem, l1_rsem, l2_ssem, l2_rsem, l3_ssem, l3_rsem,
):
    i = lax.axis_index("ctx")
    d = lax.axis_index("dp")
    g = i % PLACES
    group = i // PLACES
    parity = g % 2
    first = g // 2
    pairs = dp_size // 2
    me = g * 2 + d % 2
    planes = (ctx_size // PLACES) * pairs
    my_plane = group * pairs + d // 2

    def place_of(h):
        return (g + 2 * h) % PLACES

    def ahead(distance):
        return ((i + distance + ctx_size) % ctx_size, d)

    def plane_peer(e):
        return (group * PLACES + e // 2, (d // 2) * 2 + e % 2)

    def other_plane(r):
        return ((r // pairs) * PLACES + g, (r % pairs) * 2 + d % 2)

    def own_copies(h):
        p = place_of(h)
        cols = pl.ds(h * HALF_KEYS, HALF_KEYS)
        return [
            pltpu.make_async_copy(k_hbm.at[:, cols], k_buf.at[h, p], own_sem.at[h, 0]),
            pltpu.make_async_copy(v_hbm.at[:, cols], v_buf.at[h, p], own_sem.at[h, 1]),
            pltpu.make_async_copy(av_hbm, av_buf.at[h, p], own_sem.at[h, 2]),
        ]

    def query_copies(h):
        cols = pl.ds(pl.multiple_of(h * HALF_QUERIES, HALF_QUERIES), HALF_QUERIES)
        return [
            pltpu.make_async_copy(q_hbm.at[:, cols], q_buf.at[:, cols], load_sem.at[h, 0]),
            pltpu.make_async_copy(g_hbm.at[:, cols], g_buf.at[:, cols], load_sem.at[h, 1]),
        ]

    rank_copy = pltpu.make_async_copy(aq_hbm, aq_buf, load_sem.at[0, 2])
    for h in range(2):
        for copy in own_copies(h):
            copy.start()
    for copy in query_copies(first):
        copy.start()
    rank_copy.start()
    for copy in query_copies(1 - first):
        copy.start()

    barrier = pltpu.get_barrier_semaphore()

    def greet(device):
        pl.semaphore_signal(barrier, inc=1, device_id=device, device_id_type=MESH)

    for r in range(1, PLANE):
        greet(plane_peer((me + r) % PLANE))
    for r in range(1, planes):
        greet(other_plane((my_plane + r) % planes))
    beside = (group * PLACES + jnp.where(first == 0, -2, PLACES) + ctx_size) % ctx_size
    greet((beside, d))
    greet((beside + 1, d))
    pl.semaphore_wait(barrier, PLANE - 1 + planes - 1 + 2)

    def key_copies(h, p, distance):
        cols = pl.ds(h * HALF_KEYS, HALF_KEYS)
        target = ahead(distance)
        pieces = (
            (k_hbm.at[:, cols], k_buf.at[h, p]),
            (v_hbm.at[:, cols], v_buf.at[h, p]),
            (av_hbm, av_buf.at[h, p]),
        )
        return [
            pltpu.make_async_remote_copy(
                src_ref=src,
                dst_ref=dst,
                send_sem=kv_send.at[h, distance - 1, n],
                recv_sem=kv_recv.at[h, p, n],
                device_id=target,
                device_id_type=MESH,
            )
            for n, (src, dst) in enumerate(pieces)
        ]

    def key_arrivals(h, b):
        pieces = (k_buf.at[h, b], v_buf.at[h, b], av_buf.at[h, b])
        return [
            pltpu.make_async_remote_copy(
                src_ref=dst,
                dst_ref=dst,
                send_sem=kv_send.at[h, 0, n],
                recv_sem=kv_recv.at[h, b, n],
                device_id=ahead(1),
                device_id_type=MESH,
            )
            for n, dst in enumerate(pieces)
        ]

    for distance in range(1, PLACES):
        for h in range(2):
            p = place_of(h)

            @pl.when(p + distance < PLACES)
            def _():
                for copy in key_copies(h, p, distance):
                    copy.start()

    def return_copy(h, c, b, blocks):
        return pltpu.make_async_remote_copy(
            src_ref=part.at[h, c, b],
            dst_ref=arrived.at[h, c, blocks - 2],
            send_sem=ret_send.at[h, c, b],
            recv_sem=ret_recv.at[h, c, blocks - 2],
            device_id=ahead(b - (blocks - 1)),
            device_id_type=MESH,
        )

    def return_arrival(h, c, slot):
        return pltpu.make_async_remote_copy(
            src_ref=arrived.at[h, c, slot],
            dst_ref=arrived.at[h, c, slot],
            send_sem=ret_send.at[h, c, 0],
            recv_sem=ret_recv.at[h, c, slot],
            device_id=ahead(1),
            device_id_type=MESH,
        )

    def dq_copy(h, c):
        cols = pl.ds(pl.multiple_of((2 * h + c) * PER_HEAD * WIDTH, PER_HEAD * WIDTH), PER_HEAD * WIDTH)
        return pltpu.make_async_copy(dq_buf.at[:, cols], dq_hbm.at[:, cols], dq_sem.at[h, c])

    def head_step(h, c, blocks):
        span = blocks * ROWS
        cols = pl.ds(pl.multiple_of(c * WIDTH, WIDTH), WIDTH)
        base = (2 * h + c) * PER_HEAD * WIDTH

        def head_cols(t):
            return pl.ds(pl.multiple_of(base + t * WIDTH, WIDTH), WIDTH)

        keys = k_buf[h, :blocks, :, cols].reshape(span, WIDTH)
        vals = v_buf[h, :blocks, :, cols].reshape(span, WIDTH)
        key_row = lax.broadcasted_iota(jnp.int32, (ROWS, 2 * ROWS), 0)
        query_col = lax.broadcasted_iota(jnp.int32, (ROWS, 2 * ROWS), 1) % ROWS
        allowed = key_row <= query_col

        def pair(buf, t):
            return jnp.concatenate([buf[:, head_cols(2 * t)], buf[:, head_cols(2 * t + 1)]], axis=0)

        for t in range(PER_HEAD // 2):
            q = pair(q_buf, t)
            grad = pair(g_buf, t)
            s = matmul(keys, q, NT)
            last = jnp.where(allowed, s[span - ROWS:], -1e30)
            s = last if blocks == 1 else jnp.concatenate([s[: span - ROWS], last], axis=0)
            top = jnp.max(s, axis=0, keepdims=True)
            raised = jnp.exp2((s - top) * (SCALE * LOG2E))
            probs = raised * (1.0 / jnp.sum(raised, axis=0, keepdims=True))
            weights = probs.astype(jnp.bfloat16)
            score_grad = matmul(vals, grad, NT)
            delta = jnp.sum(weights.astype(jnp.float32) * score_grad, axis=0, keepdims=True)
            logit = (probs * (score_grad - delta)).astype(jnp.bfloat16)
            w_buf[:span, 2 * t * ROWS:(2 * t + 2) * ROWS] = weights
            l_buf[:span, 2 * t * ROWS:(2 * t + 2) * ROWS] = logit
        q_all = jnp.concatenate([q_buf[:, head_cols(t)] for t in range(PER_HEAD)], axis=0)
        grad_all = jnp.concatenate([g_buf[:, head_cols(t)] for t in range(PER_HEAD)], axis=0)
        logit_all = l_buf[:span, :]
        dk = (matmul(logit_all, q_all, NN) * SCALE).astype(jnp.bfloat16)
        dv = matmul(w_buf[:span, :], grad_all, NN).astype(jnp.bfloat16)
        for b in range(blocks):
            part[h, c, b, 0] = dk[b * ROWS:(b + 1) * ROWS]
            part[h, c, b, 1] = dv[b * ROWS:(b + 1) * ROWS]
        for b in range(blocks - 1):
            return_copy(h, c, b, blocks).start()
        dq = (matmul(logit_all, keys, TN) * SCALE).astype(jnp.bfloat16)
        for t in range(PER_HEAD):
            dq_buf[:, head_cols(t)] = dq[t * ROWS:(t + 1) * ROWS]
        dq_copy(h, c).start()
        down = aq_buf[...]
        for t in range(PER_HEAD):
            l1_send[t, 3 * h + c] = matmul(down, dq[t * ROWS:(t + 1) * ROWS], TN).astype(jnp.bfloat16)
        value_down = av_buf[h, :blocks].reshape(span, RANK)
        up = matmul(value_down, dv, TN).astype(jnp.bfloat16)
        kv = 2 * h + c
        l1_send[2 * kv, VALUE_TILE] = up
        l1_send[2 * kv + 1, VALUE_TILE] = up

    def stage(h, blocks):
        for b in range(blocks - 1):
            for copy in key_arrivals(h, b):
                copy.wait_recv()

        def one(c, carry):
            head_step(h, c, blocks)
            return carry

        lax.fori_loop(0, 2, one, 0)

    def l1_copy(n, e_from, h_from, r, target):
        start, count = (3 * h_from, 2) if n == 0 else (2 * h_from, 3)
        tiles = pl.ds(start, count)
        return pltpu.make_async_remote_copy(
            src_ref=l1_send.at[target, tiles],
            dst_ref=l1_recv.at[e_from, tiles],
            send_sem=l1_ssem.at[n, r - 1],
            recv_sem=l1_rsem.at[n, e_from],
            device_id=plane_peer(target),
            device_id_type=MESH,
        )

    def l1_start(n, h):
        for r in range(1, PLANE):
            l1_copy(n, me, h, r, (me + r) % PLANE).start()

    second = 1 - first
    for copy in own_copies(0) + own_copies(1):
        copy.wait()
    for copy in query_copies(first):
        copy.wait()
    rank_copy.wait()
    for blocks in (1, 2):
        pl.when(parity == blocks - 1)(functools.partial(stage, first, blocks))
    l1_start(0, first)
    for copy in query_copies(second):
        copy.wait()
    for blocks in (3, 4):
        pl.when(parity == blocks - 3)(functools.partial(stage, second, blocks))
    l1_start(1, second)

    total = l1_send[me].astype(jnp.float32)
    for r in range(1, PLANE):
        e = (me + r) % PLANE
        l1_copy(0, e, e // 4, r, me).wait_recv()
        l1_copy(1, e, 1 - e // 4, r, me).wait_recv()
        total = total + l1_recv[e].astype(jnp.float32)
    l2_recv[my_plane] = total.astype(jnp.bfloat16)

    def l2_copy(r, origin, target):
        return pltpu.make_async_remote_copy(
            src_ref=l2_recv.at[origin],
            dst_ref=l2_recv.at[origin],
            send_sem=l2_ssem.at[r - 1],
            recv_sem=l2_rsem.at[origin],
            device_id=other_plane(target),
            device_id_type=MESH,
        )

    for r in range(1, planes):
        l2_copy(r, my_plane, (my_plane + r) % planes).start()

    def finish(h, place):
        for c in range(2):
            for slot in range(place, PLACES - 1):
                return_arrival(h, c, slot).wait_recv()
            cols = pl.ds(pl.multiple_of((2 * h + c) * WIDTH, WIDTH), WIDTH)
            for n, out in enumerate((dk_out, dv_out)):
                acc = part[h, c, place, n].astype(jnp.float32)
                for slot in range(place, PLACES - 1):
                    acc = acc + arrived[h, c, slot, n].astype(jnp.float32)
                out[:, cols] = acc.astype(jnp.bfloat16)

    for place in (2, 3):
        pl.when(parity == place - 2)(functools.partial(finish, second, place))

    for r in range(1, planes):
        l2_copy(r, (my_plane + r) % planes, my_plane).wait_recv()
    total = l2_recv[0].astype(jnp.float32)
    for r in range(1, planes):
        total = total + l2_recv[r].astype(jnp.float32)
    l3_recv[me] = (total * ADAPTER_SCALE).astype(jnp.bfloat16)

    def l3_copy(r, origin, target):
        return pltpu.make_async_remote_copy(
            src_ref=l3_recv.at[origin],
            dst_ref=l3_recv.at[origin],
            send_sem=l3_ssem.at[r - 1],
            recv_sem=l3_rsem.at[origin],
            device_id=plane_peer(target),
            device_id_type=MESH,
        )

    for r in range(1, PLANE):
        l3_copy(r, me, (me + r) % PLANE).start()
    for place in (0, 1):
        pl.when(parity == place)(functools.partial(finish, first, place))
    for r in range(1, PLANE):
        l3_copy(r, (me + r) % PLANE, me).wait_recv()
    for e in range(PLANE):
        for kv in range(KEY_VALUE_HEADS):
            head = kv * PER_HEAD + e
            uq_out[:, head * WIDTH:(head + 1) * WIDTH] = l3_recv[e, kv + kv // 2].astype(jnp.float32)
    for kv in range(KEY_VALUE_HEADS):
        uv_out[:, kv * WIDTH:(kv + 1) * WIDTH] = l3_recv[2 * kv, VALUE_TILE].astype(jnp.float32)

    for h in range(2):
        p = place_of(h)
        for distance in range(1, PLACES):

            @pl.when(p + distance < PLACES)
            def _():
                for copy in key_copies(h, p, distance):
                    copy.wait_send()

        for c in range(2):
            dq_copy(h, c).wait()

    def returned(h, blocks):
        for c in range(2):
            for b in range(blocks - 1):
                return_copy(h, c, b, blocks).wait_send()

    pl.when(parity == 1)(functools.partial(returned, first, 2))
    for blocks in (3, 4):
        pl.when(parity == blocks - 3)(functools.partial(returned, second, blocks))
    for r in range(1, PLANE):
        l1_copy(0, me, first, r, (me + r) % PLANE).wait_send()
        l1_copy(1, me, second, r, (me + r) % PLANE).wait_send()
        l3_copy(r, me, (me + r) % PLANE).wait_send()
    for r in range(1, planes):
        l2_copy(r, my_plane, (my_plane + r) % planes).wait_send()


def body(ctx_size, dp_size, queries, keys, values, output_gradient, query_down, value_down):
    planes = (ctx_size // PLACES) * (dp_size // 2)
    bf16, f32 = jnp.bfloat16, jnp.float32
    dma = pltpu.SemaphoreType.DMA
    anywhere = pl.BlockSpec(memory_space=pl.ANY)
    vmem = pl.BlockSpec(memory_space=pltpu.VMEM)
    wide = PER_HEAD * WIDTH
    outs = pl.pallas_call(
        functools.partial(kernel, ctx_size, dp_size),
        out_shape=(
            jax.ShapeDtypeStruct(queries.shape[1:], bf16),
            jax.ShapeDtypeStruct(keys.shape[1:], bf16),
            jax.ShapeDtypeStruct(values.shape[1:], bf16),
            jax.ShapeDtypeStruct((RANK, queries.shape[2]), f32),
            jax.ShapeDtypeStruct((RANK, values.shape[2]), f32),
        ),
        in_specs=[anywhere] * 6,
        out_specs=(anywhere, vmem, vmem, vmem, vmem),
        scratch_shapes=[
            pltpu.VMEM((ROWS, KEY_VALUE_HEADS * wide), bf16),
            pltpu.VMEM((ROWS, KEY_VALUE_HEADS * wide), bf16),
            pltpu.VMEM((ROWS, RANK), bf16),
            pltpu.VMEM((ROWS, KEY_VALUE_HEADS * wide), bf16),
            pltpu.VMEM((2, PLACES, ROWS, HALF_KEYS), bf16),
            pltpu.VMEM((2, PLACES, ROWS, HALF_KEYS), bf16),
            pltpu.VMEM((2, PLACES, ROWS, RANK), bf16),
            pltpu.VMEM((PLACES * ROWS, wide), bf16),
            pltpu.VMEM((PLACES * ROWS, wide), bf16),
            pltpu.VMEM((2, 2, PLACES, 2, ROWS, WIDTH), bf16),
            pltpu.VMEM((2, 2, PLACES - 1, 2, ROWS, WIDTH), bf16),
            pltpu.VMEM((PLANE, TILES, RANK, WIDTH), bf16),
            pltpu.VMEM((PLANE, TILES, RANK, WIDTH), bf16),
            pltpu.VMEM((planes, TILES, RANK, WIDTH), bf16),
            pltpu.VMEM((PLANE, TILES, RANK, WIDTH), bf16),
            dma((2, 3)),
            dma((2, 3)),
            dma((2, 2)),
            dma((2, PLACES - 1, 3)),
            dma((2, PLACES, 3)),
            dma((2, 2, PLACES)),
            dma((2, 2, PLACES - 1)),
            dma((2, PLANE - 1)),
            dma((2, PLANE)),
            dma((max(planes - 1, 1),)),
            dma((planes,)),
            dma((PLANE - 1,)),
            dma((PLANE,)),
        ],
        compiler_params=pltpu.CompilerParams(
            collective_id=0, has_side_effects=True, vmem_limit_bytes=40 * 1024 * 1024
        ),
        cost_estimate=pl.CostEstimate(
            flops=2_500_000_000, bytes_accessed=4_000_000, transcendentals=1_600_000
        ),
    )(queries[0], keys[0], values[0], output_gradient[0], query_down[0], value_down[0])
    return (outs[0][None], outs[1][None], outs[2][None], outs[3], outs[4])


def solution(mesh):
    spec = P("dp", "ctx", None)
    return jax.shard_map(
        functools.partial(body, mesh.shape["ctx"], mesh.shape["dp"]),
        mesh=mesh,
        in_specs=(spec,) * 6,
        out_specs=(spec, spec, spec, P(), P()),
        check_vma=False,
    )
```

time: 249 us -> 50.4 us (0.20)
  waiting for transfers between devices: 95.5 us -> 0 us
  matrix products: 54.6 us -> 0 us
  Pallas kernels: 0 us -> 40.1 us
  blocking collectives: 39.8 us -> 0 us
  starting transfers between devices: 15.8 us -> 0 us
  between operations: 14.2 us -> 0.66 us
  local copies, waits for them, and re-layouts: 21.6 us -> 9.34 us
  other arithmetic: 6 us -> 0 us
    psum x1 -> x0, waiting for transfers between devices: 74.5 us -> none  [body(): lax.psum((query_adapter_term, value_adapter_term), ('ctx', 'dp'))]
    dot_general x22 -> x0, matrix products: 45.7 us -> none  [the longest x4 13.6 us: head_backward(): jnp.einsum('rts,rtd->sd', attention_weights, head_grad, preferred_element...]
    pallas_call x0 -> x1, Pallas kernels: none -> 40.1 us  [body(): pl.pallas_call(functools.partial(kernel, ctx_size, dp_size), out_shape=(j...]
    psum x1 -> x0, blocking collectives: 39.8 us -> none  [body(): lax.psum((query_adapter_term, value_adapter_term), ('ctx', 'dp'))]
    ppermute x9 -> x0, waiting for transfers between devices: 21 us -> none  [passed_along(): return lax.ppermute(block, axis, route)]
    ppermute x9 -> x0, starting transfers between devices: 15.8 us -> none  [passed_along(): return lax.ppermute(block, axis, route)]
    sub x4 -> x0, matrix products: 8.9 us -> none  [head_backward(): raised = jnp.exp(score_matrix - top)]
    dynamic_update_slice x8 -> x0, local copies, waits for them, and re-layouts: 3.65 us -> none  [attend_block(): lax.map(per_head, (query_heads.transpose(1, 2, 0, 3), grad_heads.transpos...]
  transfers between devices with their start and end apart: 10 -> 0, of which waited for: 7 -> 0; matrix products, arithmetic and copies ran while one was open for 3% -> 0% of each run, Pallas kernels for 0% -> 0%
where the time goes in v1:
time: 50.4 us; the launch traced here: 50.1 us
  Pallas kernels  40.1 us (80%)
  local copies, waits for them, and re-layouts  9.34 us (19%)
  between operations  0.66 us (1%)
    pallas_call x1, Pallas kernels, body(): pl.pallas_call(functools.partial(kernel, ctx_size, dp_size), out_shape=(j...  40.1 us
    unnamed x19, local copies, waits for them, and re-layouts  9.34 us

profile of v1, /device:TPU:0, one launch (start us, length us, event | category | flops | bytes accessed | tf_op | source)
XLA Modules:
  0.0 50.1 jit_solution(4092342990557883779)
XLA Ops:
  0.6 0.0 copy-start.4
  0.6 0.7 %copy-done.4 = bf16[1,128,16]{1,2,0:T(8,128)(2,1)S(1)} copy-done((bf16[1,128,16]{1,2,0:T(8,128)(2,1)S(1)}, bf16[1,128,16]{1,2,0:T(8,128)(2,1)}, u32[]{:S(2)}) %copy-start.4) | copy-done | bytes 4120
  1.3 0.0 copy-start.5
  1.3 0.1 copy.11
  1.4 0.6 %copy-done.5 = bf16[1,128,16]{1,2,0:T(8,128)(2,1)S(1)} copy-done((bf16[1,128,16]{1,2,0:T(8,128)(2,1)S(1)}, bf16[1,128,16]{1,2,0:T(8,128)(2,1)}, u32[]{:S(2)}) %copy-start.5) | copy-done | bytes 4120
  2.0 0.1 copy.12
  2.1 0.0 copy-start
  2.1 1.2 %copy-done = bf16[1,128,4096]{2,1,0:T(8,128)(2,1)S(1)} copy-done((bf16[1,128,4096]{2,1,0:T(8,128)(2,1)S(1)}, bf16[1,128,4096]{2,1,0:T(8,128)(2,1)}, u32[]{:S(2)}) %copy-start) | copy-done | bytes 1048600
  3.4 0.0 copy-start.1
  3.4 1.2 %copy-done.1 = bf16[1,128,4096]{2,1,0:T(8,128)(2,1)S(1)} copy-done((bf16[1,128,4096]{2,1,0:T(8,128)(2,1)S(1)}, bf16[1,128,4096]{2,1,0:T(8,128)(2,1)}, u32[]{:S(2)}) %copy-start.1) | copy-done | bytes 1048600
  4.6 0.0 copy-start.2
  4.6 0.9 %copy-done.2 = bf16[1,128,512]{2,1,0:T(8,128)(2,1)S(1)} copy-done((bf16[1,128,512]{2,1,0:T(8,128)(2,1)S(1)}, bf16[1,128,512]{2,1,0:T(8,128)(2,1)}, u32[]{:S(2)}) %copy-start.2) | copy-done | bytes 131096
  5.5 0.0 copy-start.3
  5.5 0.9 %copy-done.3 = bf16[1,128,512]{2,1,0:T(8,128)(2,1)S(1)} copy-done((bf16[1,128,512]{2,1,0:T(8,128)(2,1)S(1)}, bf16[1,128,512]{2,1,0:T(8,128)(2,1)}, u32[]{:S(2)}) %copy-start.3) | copy-done | bytes 131096
  6.4 40.1 %shard_map.101 = (bf16[128,4096]{1,0:T(8,128)(2,1)S(1)}, bf16[128,512]{1,0:T(8,128)(2,1)S(1)}, bf16[128,512]{1,0:T(8,128)(2,1)S(1)}, f32[16,4096]{1,0:T(8,128)S(1)}, f32[16,512]{1,0:T(8,128)S(1)}) custom-call(bf16[128,4096]{1,0:T(8,128)(2,1)S(1)} %bitcast.14, bf16[128,512]{1,0:T(8,128)(2,1)S(1)} %bitcast.16, bf16[128,512]{1,0:T(8,128)(2,1)S(1)} %bitcast.17, ...), custom_call_target="tpu_custom_call" | custom-call | flops 2500000000 | bytes 4000000 | tf_op jit(solution)/shard_map/pallas_call | solution.py:370
  46.5 1.0 %copy.18 = bf16[1,128,4096]{2,1,0:T(8,128)(2,1)} copy(bf16[1,128,4096]{2,1,0:T(8,128)(2,1)S(1)} %bitcast.9) | data formatting | bytes 2097152
  47.5 0.7 %copy.19 = bf16[1,128,512]{2,1,0:T(8,128)(2,1)} copy(bf16[1,128,512]{2,1,0:T(8,128)(2,1)S(1)} %bitcast.11) | data formatting | bytes 262144
  48.1 0.7 %copy.20 = bf16[1,128,512]{2,1,0:T(8,128)(2,1)} copy(bf16[1,128,512]{2,1,0:T(8,128)(2,1)S(1)} %bitcast.10) | data formatting | bytes 262144
  48.8 0.7 %copy.21 = f32[16,4096]{1,0:T(8,128)} copy(f32[16,4096]{1,0:T(8,128)S(1)} %get-tuple-element.23) | data formatting | bytes 524288
  49.5 0.6 %copy.22 = f32[16,512]{1,0:T(8,128)} copy(f32[16,512]{1,0:T(8,128)S(1)} %get-tuple-element.24) | data formatting | bytes 65536
Async XLA Ops:
  0.6 0.7 %copy-start.4 = (bf16[1,128,16]{1,2,0:T(8,128)(2,1)S(1)}, bf16[1,128,16]{1,2,0:T(8,128)(2,1)}, u32[]{:S(2)}) copy-start(bf16[1,128,16]{1,2,0:T(8,128)(2,1)} %param.10) | copy-start | bytes 12292
  1.3 0.7 %copy-start.5 = (bf16[1,128,16]{1,2,0:T(8,128)(2,1)S(1)}, bf16[1,128,16]{1,2,0:T(8,128)(2,1)}, u32[]{:S(2)}) copy-start(bf16[1,128,16]{1,2,0:T(8,128)(2,1)} %param.11) | copy-start | bytes 12292
  2.1 1.2 %copy-start = (bf16[1,128,4096]{2,1,0:T(8,128)(2,1)S(1)}, bf16[1,128,4096]{2,1,0:T(8,128)(2,1)}, u32[]{:S(2)}) copy-start(bf16[1,128,4096]{2,1,0:T(8,128)(2,1)} %param.6) | copy-start | bytes 3145732
  3.4 1.2 %copy-start.1 = (bf16[1,128,4096]{2,1,0:T(8,128)(2,1)S(1)}, bf16[1,128,4096]{2,1,0:T(8,128)(2,1)}, u32[]{:S(2)}) copy-start(bf16[1,128,4096]{2,1,0:T(8,128)(2,1)} %param.9) | copy-start | bytes 3145732
  4.6 0.9 %copy-start.2 = (bf16[1,128,512]{2,1,0:T(8,128)(2,1)S(1)}, bf16[1,128,512]{2,1,0:T(8,128)(2,1)}, u32[]{:S(2)}) copy-start(bf16[1,128,512]{2,1,0:T(8,128)(2,1)} %param.7) | copy-start | bytes 393220
  5.5 0.9 %copy-start.3 = (bf16[1,128,512]{2,1,0:T(8,128)(2,1)S(1)}, bf16[1,128,512]{2,1,0:T(8,128)(2,1)}, u32[]{:S(2)}) copy-start(bf16[1,128,512]{2,1,0:T(8,128)(2,1)} %param.8) | copy-start | bytes 393220

commit v2 on v1

--- a/solution.py
+++ b/solution.py
@@ -17,13 +17,15 @@
 HALF_QUERIES = 2048
 PLANE = 8
 TILES = 5
+KEY_ROWS = slice(0, ROWS)
+VALUE_ROWS = slice(ROWS, 2 * ROWS)
+DOWN_ROWS = slice(2 * ROWS, 2 * ROWS + RANK)
 VALUE_TILE = 2
 ADAPTER_SCALE = 2.0
 SCALE = WIDTH ** (-0.5)
 LOG2E = 1.4426950408889634
 MESH = pl.DeviceIdType.MESH
 NT = (((1,), (1,)), ((), ()))
-TN = (((0,), (0,)), ((), ()))
 NN = (((1,), (0,)), ((), ()))
 
 
@@ -34,10 +36,10 @@
 def kernel(
     ctx_size, dp_size,
     q_hbm, k_hbm, v_hbm, g_hbm, aq_hbm, av_hbm,
-    dq_hbm, dk_out, dv_out, uq_out, uv_out,
-    q_buf, g_buf, aq_buf, dq_buf, k_buf, v_buf, av_buf, w_buf, l_buf,
+    dq_out, dk_out, dv_out, uq_out, uv_out,
+    q_buf, g_buf, aq_buf, kv_buf, w_buf, l_buf,
     part, arrived, l1_send, l1_recv, l2_recv, l3_recv,
-    load_sem, own_sem, dq_sem, kv_send, kv_recv, ret_send, ret_recv,
+    load_sem, own_sem, kv_send, kv_recv, ret_send, ret_recv,
     l1_ssem, l1_rsem, l2_ssem, l2_rsem, l3_ssem, l3_rsem,
 ):
     i = lax.axis_index("ctx")
@@ -67,9 +69,9 @@
         p = place_of(h)
         cols = pl.ds(h * HALF_KEYS, HALF_KEYS)
         return [
-            pltpu.make_async_copy(k_hbm.at[:, cols], k_buf.at[h, p], own_sem.at[h, 0]),
-            pltpu.make_async_copy(v_hbm.at[:, cols], v_buf.at[h, p], own_sem.at[h, 1]),
-            pltpu.make_async_copy(av_hbm, av_buf.at[h, p], own_sem.at[h, 2]),
+            pltpu.make_async_copy(k_hbm.at[:, cols], kv_buf.at[h, p, KEY_ROWS], own_sem.at[h, 0]),
+            pltpu.make_async_copy(v_hbm.at[:, cols], kv_buf.at[h, p, VALUE_ROWS], own_sem.at[h, 1]),
+            pltpu.make_async_copy(av_hbm, kv_buf.at[h, p, DOWN_ROWS, pl.ds(0, ROWS)], own_sem.at[h, 2]),
         ]
 
     def query_copies(h):
@@ -103,48 +105,35 @@
     greet((beside + 1, d))
     pl.semaphore_wait(barrier, PLANE - 1 + planes - 1 + 2)
 
-    def key_copies(h, p, distance):
-        cols = pl.ds(h * HALF_KEYS, HALF_KEYS)
-        target = ahead(distance)
-        pieces = (
-            (k_hbm.at[:, cols], k_buf.at[h, p]),
-            (v_hbm.at[:, cols], v_buf.at[h, p]),
-            (av_hbm, av_buf.at[h, p]),
-        )
-        return [
-            pltpu.make_async_remote_copy(
-                src_ref=src,
-                dst_ref=dst,
-                send_sem=kv_send.at[h, distance - 1, n],
-                recv_sem=kv_recv.at[h, p, n],
-                device_id=target,
-                device_id_type=MESH,
-            )
-            for n, (src, dst) in enumerate(pieces)
-        ]
-
-    def key_arrivals(h, b):
-        pieces = (k_buf.at[h, b], v_buf.at[h, b], av_buf.at[h, b])
-        return [
-            pltpu.make_async_remote_copy(
-                src_ref=dst,
-                dst_ref=dst,
-                send_sem=kv_send.at[h, 0, n],
-                recv_sem=kv_recv.at[h, b, n],
-                device_id=ahead(1),
-                device_id_type=MESH,
-            )
-            for n, dst in enumerate(pieces)
-        ]
-
+    def key_copy(h, p, distance):
+        return pltpu.make_async_remote_copy(
+            src_ref=kv_buf.at[h, p],
+            dst_ref=kv_buf.at[h, p],
+            send_sem=kv_send.at[h, distance - 1],
+            recv_sem=kv_recv.at[h, p],
+            device_id=ahead(distance),
+            device_id_type=MESH,
+        )
+
+    def key_arrival(h, b):
+        return pltpu.make_async_remote_copy(
+            src_ref=kv_buf.at[h, b],
+            dst_ref=kv_buf.at[h, b],
+            send_sem=kv_send.at[h, 0],
+            recv_sem=kv_recv.at[h, b],
+            device_id=ahead(1),
+            device_id_type=MESH,
+        )
+
+    for copy in own_copies(0) + own_copies(1):
+        copy.wait()
     for distance in range(1, PLACES):
         for h in range(2):
             p = place_of(h)
 
             @pl.when(p + distance < PLACES)
             def _():
-                for copy in key_copies(h, p, distance):
-                    copy.start()
+                key_copy(h, p, distance).start()
 
     def return_copy(h, c, b, blocks):
         return pltpu.make_async_remote_copy(
@@ -166,10 +155,6 @@
             device_id_type=MESH,
         )
 
-    def dq_copy(h, c):
-        cols = pl.ds(pl.multiple_of((2 * h + c) * PER_HEAD * WIDTH, PER_HEAD * WIDTH), PER_HEAD * WIDTH)
-        return pltpu.make_async_copy(dq_buf.at[:, cols], dq_hbm.at[:, cols], dq_sem.at[h, c])
-
     def head_step(h, c, blocks):
         span = blocks * ROWS
         cols = pl.ds(pl.multiple_of(c * WIDTH, WIDTH), WIDTH)
@@ -178,8 +163,8 @@
         def head_cols(t):
             return pl.ds(pl.multiple_of(base + t * WIDTH, WIDTH), WIDTH)
 
-        keys = k_buf[h, :blocks, :, cols].reshape(span, WIDTH)
-        vals = v_buf[h, :blocks, :, cols].reshape(span, WIDTH)
+        keys = kv_buf[h, :blocks, KEY_ROWS, cols].reshape(span, WIDTH)
+        vals = kv_buf[h, :blocks, VALUE_ROWS, cols].reshape(span, WIDTH)
         key_row = lax.broadcasted_iota(jnp.int32, (ROWS, 2 * ROWS), 0)
         query_col = lax.broadcasted_iota(jnp.int32, (ROWS, 2 * ROWS), 1) % ROWS
         allowed = key_row <= query_col
@@ -194,11 +179,12 @@
             last = jnp.where(allowed, s[span - ROWS:], -1e30)
             s = last if blocks == 1 else jnp.concatenate([s[: span - ROWS], last], axis=0)
             top = jnp.max(s, axis=0, keepdims=True)
+            score_grad = matmul(vals, grad, NT)
             raised = jnp.exp2((s - top) * (SCALE * LOG2E))
-            probs = raised * (1.0 / jnp.sum(raised, axis=0, keepdims=True))
+            inverse = 1.0 / jnp.sum(raised, axis=0, keepdims=True)
+            delta = jnp.sum(raised * score_grad, axis=0, keepdims=True) * inverse
+            probs = raised * inverse
             weights = probs.astype(jnp.bfloat16)
-            score_grad = matmul(vals, grad, NT)
-            delta = jnp.sum(weights.astype(jnp.float32) * score_grad, axis=0, keepdims=True)
             logit = (probs * (score_grad - delta)).astype(jnp.bfloat16)
             w_buf[:span, 2 * t * ROWS:(2 * t + 2) * ROWS] = weights
             l_buf[:span, 2 * t * ROWS:(2 * t + 2) * ROWS] = logit
@@ -212,23 +198,22 @@
             part[h, c, b, 1] = dv[b * ROWS:(b + 1) * ROWS]
         for b in range(blocks - 1):
             return_copy(h, c, b, blocks).start()
-        dq = (matmul(logit_all, keys, TN) * SCALE).astype(jnp.bfloat16)
+        dq = (matmul(keys.T, logit_all, NN) * SCALE).astype(jnp.bfloat16)
         for t in range(PER_HEAD):
-            dq_buf[:, head_cols(t)] = dq[t * ROWS:(t + 1) * ROWS]
-        dq_copy(h, c).start()
-        down = aq_buf[...]
+            dq_out[:, head_cols(t)] = dq[:, t * ROWS:(t + 1) * ROWS].T
+        wide = pl.ds(pl.multiple_of(base, PER_HEAD * WIDTH), PER_HEAD * WIDTH)
+        up = matmul(aq_buf[...], dq_out[:, wide], NN).astype(jnp.bfloat16)
         for t in range(PER_HEAD):
-            l1_send[t, 3 * h + c] = matmul(down, dq[t * ROWS:(t + 1) * ROWS], TN).astype(jnp.bfloat16)
-        value_down = av_buf[h, :blocks].reshape(span, RANK)
-        up = matmul(value_down, dv, TN).astype(jnp.bfloat16)
+            l1_send[t, 3 * h + c] = up[:, t * WIDTH:(t + 1) * WIDTH]
+        value_down = jnp.concatenate([kv_buf[h, b, DOWN_ROWS, :ROWS] for b in range(blocks)], axis=1)
+        up = matmul(value_down, dv, NN).astype(jnp.bfloat16)
         kv = 2 * h + c
         l1_send[2 * kv, VALUE_TILE] = up
         l1_send[2 * kv + 1, VALUE_TILE] = up
 
     def stage(h, blocks):
         for b in range(blocks - 1):
-            for copy in key_arrivals(h, b):
-                copy.wait_recv()
+            key_arrival(h, b).wait_recv()
 
         def one(c, carry):
             head_step(h, c, blocks)
@@ -236,42 +221,33 @@
 
         lax.fori_loop(0, 2, one, 0)
 
-    def l1_copy(n, e_from, h_from, r, target):
-        start, count = (3 * h_from, 2) if n == 0 else (2 * h_from, 3)
-        tiles = pl.ds(start, count)
-        return pltpu.make_async_remote_copy(
-            src_ref=l1_send.at[target, tiles],
-            dst_ref=l1_recv.at[e_from, tiles],
-            send_sem=l1_ssem.at[n, r - 1],
-            recv_sem=l1_rsem.at[n, e_from],
+    def l1_copy(r, origin, target):
+        return pltpu.make_async_remote_copy(
+            src_ref=l1_send.at[target],
+            dst_ref=l1_recv.at[origin],
+            send_sem=l1_ssem.at[r - 1],
+            recv_sem=l1_rsem.at[origin],
             device_id=plane_peer(target),
             device_id_type=MESH,
         )
 
-    def l1_start(n, h):
-        for r in range(1, PLANE):
-            l1_copy(n, me, h, r, (me + r) % PLANE).start()
-
     second = 1 - first
-    for copy in own_copies(0) + own_copies(1):
-        copy.wait()
     for copy in query_copies(first):
         copy.wait()
     rank_copy.wait()
     for blocks in (1, 2):
         pl.when(parity == blocks - 1)(functools.partial(stage, first, blocks))
-    l1_start(0, first)
     for copy in query_copies(second):
         copy.wait()
     for blocks in (3, 4):
         pl.when(parity == blocks - 3)(functools.partial(stage, second, blocks))
-    l1_start(1, second)
+    for r in range(1, PLANE):
+        l1_copy(r, me, (me + r) % PLANE).start()
 
     total = l1_send[me].astype(jnp.float32)
     for r in range(1, PLANE):
         e = (me + r) % PLANE
-        l1_copy(0, e, e // 4, r, me).wait_recv()
-        l1_copy(1, e, 1 - e // 4, r, me).wait_recv()
+        l1_copy(r, e, me).wait_recv()
         total = total + l1_recv[e].astype(jnp.float32)
     l2_recv[my_plane] = total.astype(jnp.bfloat16)
 
@@ -338,11 +314,7 @@
 
             @pl.when(p + distance < PLACES)
             def _():
-                for copy in key_copies(h, p, distance):
-                    copy.wait_send()
-
-        for c in range(2):
-            dq_copy(h, c).wait()
+                key_copy(h, p, distance).wait_send()
 
     def returned(h, blocks):
         for c in range(2):
@@ -353,18 +325,29 @@
     for blocks in (3, 4):
         pl.when(parity == blocks - 3)(functools.partial(returned, second, blocks))
     for r in range(1, PLANE):
-        l1_copy(0, me, first, r, (me + r) % PLANE).wait_send()
-        l1_copy(1, me, second, r, (me + r) % PLANE).wait_send()
+        l1_copy(r, me, (me + r) % PLANE).wait_send()
         l3_copy(r, me, (me + r) % PLANE).wait_send()
     for r in range(1, planes):
         l2_copy(r, my_plane, (my_plane + r) % planes).wait_send()
+
+
+def write_out(*refs):
+    sources, targets, sems = refs[:5], refs[5:10], refs[10]
+    copies = [
+        pltpu.make_async_copy(source, target, sems.at[n])
+        for n, (source, target) in enumerate(zip(sources, targets))
+    ]
+    for copy in copies:
+        copy.start()
+    for copy in copies:
+        copy.wait()
 
 
 def body(ctx_size, dp_size, queries, keys, values, output_gradient, query_down, value_down):
     planes = (ctx_size // PLACES) * (dp_size // 2)
     bf16, f32 = jnp.bfloat16, jnp.float32
     dma = pltpu.SemaphoreType.DMA
-    anywhere = pl.BlockSpec(memory_space=pl.ANY)
+    hbm = pl.BlockSpec(memory_space=pltpu.HBM)
     vmem = pl.BlockSpec(memory_space=pltpu.VMEM)
     wide = PER_HEAD * WIDTH
     outs = pl.pallas_call(
@@ -376,16 +359,13 @@
             jax.ShapeDtypeStruct((RANK, queries.shape[2]), f32),
             jax.ShapeDtypeStruct((RANK, values.shape[2]), f32),
         ),
-        in_specs=[anywhere] * 6,
-        out_specs=(anywhere, vmem, vmem, vmem, vmem),
+        in_specs=[hbm] * 6,
+        out_specs=(vmem,) * 5,
         scratch_shapes=[
             pltpu.VMEM((ROWS, KEY_VALUE_HEADS * wide), bf16),
             pltpu.VMEM((ROWS, KEY_VALUE_HEADS * wide), bf16),
-            pltpu.VMEM((ROWS, RANK), bf16),
-            pltpu.VMEM((ROWS, KEY_VALUE_HEADS * wide), bf16),
-            pltpu.VMEM((2, PLACES, ROWS, HALF_KEYS), bf16),
-            pltpu.VMEM((2, PLACES, ROWS, HALF_KEYS), bf16),
-            pltpu.VMEM((2, PLACES, ROWS, RANK), bf16),
+            pltpu.VMEM((RANK, ROWS), bf16),
+            pltpu.VMEM((2, PLACES, 2 * ROWS + RANK, HALF_KEYS), bf16),
             pltpu.VMEM((PLACES * ROWS, wide), bf16),
             pltpu.VMEM((PLACES * ROWS, wide), bf16),
             pltpu.VMEM((2, 2, PLACES, 2, ROWS, WIDTH), bf16),
@@ -396,13 +376,12 @@
             pltpu.VMEM((PLANE, TILES, RANK, WIDTH), bf16),
             dma((2, 3)),
             dma((2, 3)),
-            dma((2, 2)),
-            dma((2, PLACES - 1, 3)),
-            dma((2, PLACES, 3)),
+            dma((2, PLACES - 1)),
+            dma((2, PLACES)),
             dma((2, 2, PLACES)),
             dma((2, 2, PLACES - 1)),
-            dma((2, PLANE - 1)),
-            dma((2, PLANE)),
+            dma((PLANE - 1,)),
+            dma((PLANE,)),
             dma((max(planes - 1, 1),)),
             dma((planes,)),
             dma((PLANE - 1,)),
@@ -414,7 +393,14 @@
         cost_estimate=pl.CostEstimate(
             flops=2_500_000_000, bytes_accessed=4_000_000, transcendentals=1_600_000
         ),
-    )(queries[0], keys[0], values[0], output_gradient[0], query_down[0], value_down[0])
+    )(*[pltpu.with_memory_space_constraint(x, pltpu.HBM) for x in (queries[0], keys[0], values[0], output_gradient[0], query_down[0].T, value_down[0].T)])
+    outs = pl.pallas_call(
+        write_out,
+        out_shape=tuple(jax.ShapeDtypeStruct(x.shape, x.dtype) for x in outs),
+        in_specs=[vmem] * 5,
+        out_specs=(hbm,) * 5,
+        scratch_shapes=[dma((5,))],
+    )(*outs)
     return (outs[0][None], outs[1][None], outs[2][None], outs[3], outs[4])
 
 

time: 50.4 us -> 45 us (0.89)
  local copies, waits for them, and re-layouts: 9.34 us -> 3.59 us
    unnamed x19 -> x10, local copies, waits for them, and re-layouts: 9.34 us -> 3.59 us
    pallas_call x0 -> x1, Pallas kernels: none -> 2.56 us  [body(): pl.pallas_call(write_out, out_shape=tuple((jax.ShapeDtypeStruct(x.shape,...]
    pallas_call x1, Pallas kernels: 40.1 us -> 38 us  [body(): pl.pallas_call(functools.partial(kernel, ctx_size, dp_size), out_shape=(j...]
where the time goes in v2:
time: 45 us; the launch traced here: 44.8 us
  Pallas kernels  40.6 us (90%)
  local copies, waits for them, and re-layouts  3.59 us (8%)
  between operations  0.65 us (1%)
    pallas_call x1, Pallas kernels, body(): pl.pallas_call(functools.partial(kernel, ctx_size, dp_size), out_shape=(j...  38 us
    unnamed x10, local copies, waits for them, and re-layouts  3.59 us
    pallas_call x1, Pallas kernels, body(): pl.pallas_call(write_out, out_shape=tuple((jax.ShapeDtypeStruct(x.shape,...  2.56 us

profile of v2, /device:TPU:0, one launch (start us, length us, event | category | flops | bytes accessed | tf_op | source)
XLA Modules:
  0.0 44.8 jit_solution(5971532089179629851)
XLA Ops:
  0.6 38.0 %shard_map.101 = (bf16[128,4096]{1,0:T(8,128)(2,1)S(1)}, bf16[128,512]{1,0:T(8,128)(2,1)S(1)}, bf16[128,512]{1,0:T(8,128)(2,1)S(1)}, f32[16,4096]{1,0:T(8,128)S(1)}, f32[16,512]{1,0:T(8,128)S(1)}) custom-call(bf16[128,4096]{1,0:T(8,128)(2,1)} %bitcast.13, bf16[128,512]{1,0:T(8,128)(2,1)} %bitcast.16, bf16[128,512]{1,0:T(8,128)(2,1)} %bitcast.17, ...), custom_call_target="tpu_custom_call" | custom-call | flops 2500000000 | bytes 4000000 | tf_op jit(solution)/shard_map/pallas_call | solution.py:353
  38.6 0.0 copy-start
  38.6 1.0 %copy-done = bf16[128,4096]{1,0:T(8,128)(2,1)} copy-done((bf16[128,4096]{1,0:T(8,128)(2,1)}, bf16[128,4096]{1,0:T(8,128)(2,1)S(1)}, u32[]{:S(2)}) %copy-start) | copy-done | bytes 1048600
  39.6 0.0 copy-start.1
  39.6 0.7 %copy-done.1 = f32[16,4096]{1,0:T(8,128)} copy-done((f32[16,4096]{1,0:T(8,128)}, f32[16,4096]{1,0:T(8,128)S(1)}, u32[]{:S(2)}) %copy-start.1) | copy-done | bytes 262168
  40.3 0.0 copy-start.2
  40.3 0.7 %copy-done.2 = bf16[128,512]{1,0:T(8,128)(2,1)} copy-done((bf16[128,512]{1,0:T(8,128)(2,1)}, bf16[128,512]{1,0:T(8,128)(2,1)S(1)}, u32[]{:S(2)}) %copy-start.2) | copy-done | bytes 131096
  41.0 0.0 copy-start.3
  41.0 0.6 %copy-done.3 = bf16[128,512]{1,0:T(8,128)(2,1)} copy-done((bf16[128,512]{1,0:T(8,128)(2,1)}, bf16[128,512]{1,0:T(8,128)(2,1)S(1)}, u32[]{:S(2)}) %copy-start.3) | copy-done | bytes 131096
  41.6 0.0 copy-start.4
  41.6 0.6 %copy-done.4 = f32[16,512]{1,0:T(8,128)} copy-done((f32[16,512]{1,0:T(8,128)}, f32[16,512]{1,0:T(8,128)S(1)}, u32[]{:S(2)}) %copy-start.4) | copy-done | bytes 32792
  42.2 2.6 %shard_map.102 = (bf16[128,4096]{1,0:T(8,128)(2,1)}, bf16[128,512]{1,0:T(8,128)(2,1)}, bf16[128,512]{1,0:T(8,128)(2,1)}, f32[16,4096]{1,0:T(8,128)}, f32[16,512]{1,0:T(8,128)}) custom-call(bf16[128,4096]{1,0:T(8,128)(2,1)} %copy-done, bf16[128,512]{1,0:T(8,128)(2,1)} %copy-done.2, bf16[128,512]{1,0:T(8,128)(2,1)} %copy-done.3, f32[16,4096]{1,0:T(8,128)} %copy-done.1, ...), custom_call_target="tpu_custom_call" | custom-call | tf_op jit(solution)/shard_map/pallas_call | solution.py:397
Async XLA Ops:
  38.6 1.0 %copy-start = (bf16[128,4096]{1,0:T(8,128)(2,1)}, bf16[128,4096]{1,0:T(8,128)(2,1)S(1)}, u32[]{:S(2)}) copy-start(bf16[128,4096]{1,0:T(8,128)(2,1)S(1)} %get-tuple-element.15.refs_0_) | copy-start | bytes 3145732
  39.6 0.7 %copy-start.1 = (f32[16,4096]{1,0:T(8,128)}, f32[16,4096]{1,0:T(8,128)S(1)}, u32[]{:S(2)}) copy-start(f32[16,4096]{1,0:T(8,128)S(1)} %get-tuple-element.18.refs_3_) | copy-start | bytes 786436
  40.3 0.7 %copy-start.2 = (bf16[128,512]{1,0:T(8,128)(2,1)}, bf16[128,512]{1,0:T(8,128)(2,1)S(1)}, u32[]{:S(2)}) copy-start(bf16[128,512]{1,0:T(8,128)(2,1)S(1)} %get-tuple-element.16.refs_1_) | copy-start | bytes 393220
  41.0 0.7 %copy-start.3 = (bf16[128,512]{1,0:T(8,128)(2,1)}, bf16[128,512]{1,0:T(8,128)(2,1)S(1)}, u32[]{:S(2)}) copy-start(bf16[128,512]{1,0:T(8,128)(2,1)S(1)} %get-tuple-element.17.refs_2_) | copy-start | bytes 393220
  41.6 0.6 %copy-start.4 = (f32[16,512]{1,0:T(8,128)}, f32[16,512]{1,0:T(8,128)S(1)}, u32[]{:S(2)}) copy-start(f32[16,512]{1,0:T(8,128)S(1)} %get-tuple-element.19.refs_4_) | copy-start | bytes 98308

commit v3 on v2

--- a/solution.py
+++ b/solution.py
@@ -48,6 +48,7 @@
     group = i // PLACES
     parity = g % 2
     first = g // 2
+    second = 1 - first
     pairs = dp_size // 2
     me = g * 2 + d % 2
     planes = (ctx_size // PLACES) * pairs
@@ -67,7 +68,7 @@
 
     def own_copies(h):
         p = place_of(h)
-        cols = pl.ds(h * HALF_KEYS, HALF_KEYS)
+        cols = pl.ds(pl.multiple_of(h * HALF_KEYS, HALF_KEYS), HALF_KEYS)
         return [
             pltpu.make_async_copy(k_hbm.at[:, cols], kv_buf.at[h, p, KEY_ROWS], own_sem.at[h, 0]),
             pltpu.make_async_copy(v_hbm.at[:, cols], kv_buf.at[h, p, VALUE_ROWS], own_sem.at[h, 1]),
@@ -82,13 +83,13 @@
         ]
 
     rank_copy = pltpu.make_async_copy(aq_hbm, aq_buf, load_sem.at[0, 2])
-    for h in range(2):
+    for h in (first, second):
         for copy in own_copies(h):
             copy.start()
     for copy in query_copies(first):
         copy.start()
     rank_copy.start()
-    for copy in query_copies(1 - first):
+    for copy in query_copies(second):
         copy.start()
 
     barrier = pltpu.get_barrier_semaphore()
@@ -125,10 +126,20 @@
             device_id_type=MESH,
         )
 
-    for copy in own_copies(0) + own_copies(1):
+    def relay(h):
+        return pltpu.make_async_remote_copy(
+            src_ref=kv_buf.at[h, 0],
+            dst_ref=kv_buf.at[h, 0],
+            send_sem=kv_send.at[h, 2],
+            recv_sem=kv_recv.at[h, 0],
+            device_id=ahead(2),
+            device_id_type=MESH,
+        )
+
+    for copy in own_copies(first) + own_copies(second):
         copy.wait()
-    for distance in range(1, PLACES):
-        for h in range(2):
+    for distance in range(1, PLACES - 1):
+        for h in (first, second):
             p = place_of(h)
 
             @pl.when(p + distance < PLACES)
@@ -154,6 +165,20 @@
             device_id=ahead(1),
             device_id_type=MESH,
         )
+
+    def l1_copy(r, origin, target):
+        return pltpu.make_async_remote_copy(
+            src_ref=l1_send.at[target],
+            dst_ref=l1_recv.at[origin],
+            send_sem=l1_ssem.at[r - 1],
+            recv_sem=l1_rsem.at[origin],
+            device_id=plane_peer(target),
+            device_id_type=MESH,
+        )
+
+    def l1_start():
+        for r in range(1, PLANE):
+            l1_copy(r, me, (me + r) % PLANE).start()
 
     def head_step(h, c, blocks):
         span = blocks * ROWS
@@ -191,13 +216,7 @@
         q_all = jnp.concatenate([q_buf[:, head_cols(t)] for t in range(PER_HEAD)], axis=0)
         grad_all = jnp.concatenate([g_buf[:, head_cols(t)] for t in range(PER_HEAD)], axis=0)
         logit_all = l_buf[:span, :]
-        dk = (matmul(logit_all, q_all, NN) * SCALE).astype(jnp.bfloat16)
         dv = matmul(w_buf[:span, :], grad_all, NN).astype(jnp.bfloat16)
-        for b in range(blocks):
-            part[h, c, b, 0] = dk[b * ROWS:(b + 1) * ROWS]
-            part[h, c, b, 1] = dv[b * ROWS:(b + 1) * ROWS]
-        for b in range(blocks - 1):
-            return_copy(h, c, b, blocks).start()
         dq = (matmul(keys.T, logit_all, NN) * SCALE).astype(jnp.bfloat16)
         for t in range(PER_HEAD):
             dq_out[:, head_cols(t)] = dq[:, t * ROWS:(t + 1) * ROWS].T
@@ -210,10 +229,20 @@
         kv = 2 * h + c
         l1_send[2 * kv, VALUE_TILE] = up
         l1_send[2 * kv + 1, VALUE_TILE] = up
+        if blocks > 2:
+            pl.when(c == 1)(l1_start)
+        dk = (matmul(logit_all, q_all, NN) * SCALE).astype(jnp.bfloat16)
+        for b in range(blocks):
+            part[h, c, b, 0] = dk[b * ROWS:(b + 1) * ROWS]
+            part[h, c, b, 1] = dv[b * ROWS:(b + 1) * ROWS]
+        for b in range(blocks - 1):
+            return_copy(h, c, b, blocks).start()
 
     def stage(h, blocks):
         for b in range(blocks - 1):
             key_arrival(h, b).wait_recv()
+        if blocks == 2:
+            relay(h).start()
 
         def one(c, carry):
             head_step(h, c, blocks)
@@ -221,17 +250,6 @@
 
         lax.fori_loop(0, 2, one, 0)
 
-    def l1_copy(r, origin, target):
-        return pltpu.make_async_remote_copy(
-            src_ref=l1_send.at[target],
-            dst_ref=l1_recv.at[origin],
-            send_sem=l1_ssem.at[r - 1],
-            recv_sem=l1_rsem.at[origin],
-            device_id=plane_peer(target),
-            device_id_type=MESH,
-        )
-
-    second = 1 - first
     for copy in query_copies(first):
         copy.wait()
     rank_copy.wait()
@@ -241,8 +259,6 @@
         copy.wait()
     for blocks in (3, 4):
         pl.when(parity == blocks - 3)(functools.partial(stage, second, blocks))
-    for r in range(1, PLANE):
-        l1_copy(r, me, (me + r) % PLANE).start()
 
     total = l1_send[me].astype(jnp.float32)
     for r in range(1, PLANE):
@@ -308,9 +324,10 @@
     for kv in range(KEY_VALUE_HEADS):
         uv_out[:, kv * WIDTH:(kv + 1) * WIDTH] = l3_recv[2 * kv, VALUE_TILE].astype(jnp.float32)
 
-    for h in range(2):
+    pl.when(parity == 1)(lambda: relay(first).wait_send())
+    for h in (first, second):
         p = place_of(h)
-        for distance in range(1, PLACES):
+        for distance in range(1, PLACES - 1):
 
             @pl.when(p + distance < PLACES)
             def _():
@@ -353,11 +370,11 @@
     outs = pl.pallas_call(
         functools.partial(kernel, ctx_size, dp_size),
         out_shape=(
-            jax.ShapeDtypeStruct(queries.shape[1:], bf16),
-            jax.ShapeDtypeStruct(keys.shape[1:], bf16),
-            jax.ShapeDtypeStruct(values.shape[1:], bf16),
-            jax.ShapeDtypeStruct((RANK, queries.shape[2]), f32),
-            jax.ShapeDtypeStruct((RANK, values.shape[2]), f32),
+            pltpu.VMEM(queries.shape[1:], bf16),
+            pltpu.VMEM(keys.shape[1:], bf16),
+            pltpu.VMEM(values.shape[1:], bf16),
+            pltpu.VMEM((RANK, queries.shape[2]), f32),
+            pltpu.VMEM((RANK, values.shape[2]), f32),
         ),
         in_specs=[hbm] * 6,
         out_specs=(vmem,) * 5,
@@ -400,7 +417,7 @@
         in_specs=[vmem] * 5,
         out_specs=(hbm,) * 5,
         scratch_shapes=[dma((5,))],
-    )(*outs)
+    )(*[pltpu.with_memory_space_constraint(x, pltpu.VMEM) for x in outs])
     return (outs[0][None], outs[1][None], outs[2][None], outs[3], outs[4])
 
 

time: 45 us -> 36.5 us (0.81)
  Pallas kernels: 40.6 us -> 35.7 us
  local copies, waits for them, and re-layouts: 3.59 us -> 0 us
    unnamed x10 -> x0, local copies, waits for them, and re-layouts: 3.59 us -> none
    pallas_call x1, Pallas kernels: 38 us -> 34.5 us  [body(): pl.pallas_call(functools.partial(kernel, ctx_size, dp_size), out_shape=(p...]
    pallas_call x1, Pallas kernels: 2.56 us -> 1.18 us  [body(): pl.pallas_call(write_out, out_shape=tuple((jax.ShapeDtypeStruct(x.shape,...]
where the time goes in v3:
time: 36.5 us; the launch traced here: 36.3 us
  Pallas kernels  35.7 us (98%)
  between operations  0.64 us (2%)
    pallas_call x1, Pallas kernels, body(): pl.pallas_call(functools.partial(kernel, ctx_size, dp_size), out_shape=(p...  34.5 us
    pallas_call x1, Pallas kernels, body(): pl.pallas_call(write_out, out_shape=tuple((jax.ShapeDtypeStruct(x.shape,...  1.18 us

profile of v3, /device:TPU:0, one launch (start us, length us, event | category | flops | bytes accessed | tf_op | source)
XLA Modules:
  0.0 36.3 jit_solution(13631774642936980899)
XLA Ops:
  0.6 34.5 %shard_map.101 = (bf16[128,4096]{1,0:T(8,128)(2,1)S(1)}, bf16[128,512]{1,0:T(8,128)(2,1)S(1)}, bf16[128,512]{1,0:T(8,128)(2,1)S(1)}, f32[16,4096]{1,0:T(8,128)S(1)}, f32[16,512]{1,0:T(8,128)S(1)}) custom-call(bf16[128,4096]{1,0:T(8,128)(2,1)} %bitcast.13, bf16[128,512]{1,0:T(8,128)(2,1)} %bitcast.16, bf16[128,512]{1,0:T(8,128)(2,1)} %bitcast.17, ...), custom_call_target="tpu_custom_call" | custom-call | flops 2500000000 | bytes 4000000 | tf_op jit(solution)/shard_map/pallas_call | solution.py:370
  35.1 1.2 %shard_map.102 = (bf16[128,4096]{1,0:T(8,128)(2,1)}, bf16[128,512]{1,0:T(8,128)(2,1)}, bf16[128,512]{1,0:T(8,128)(2,1)}, f32[16,4096]{1,0:T(8,128)}, f32[16,512]{1,0:T(8,128)}) custom-call(bf16[128,4096]{1,0:T(8,128)(2,1)S(1)} %get-tuple-element.15.refs_0_, bf16[128,512]{1,0:T(8,128)(2,1)S(1)} %get-tuple-element.16.refs_1_, ...), custom_call_target="tpu_custom_call" | custom-call | tf_op jit(solution)/shard_map/pallas_call | solution.py:414

commit v4 on v3

--- a/solution.py
+++ b/solution.py
@@ -197,7 +197,7 @@
         def pair(buf, t):
             return jnp.concatenate([buf[:, head_cols(2 * t)], buf[:, head_cols(2 * t + 1)]], axis=0)
 
-        for t in range(PER_HEAD // 2):
+        def pair_step(t, carry):
             q = pair(q_buf, t)
             grad = pair(g_buf, t)
             s = matmul(keys, q, NT)
@@ -211,8 +211,12 @@
             probs = raised * inverse
             weights = probs.astype(jnp.bfloat16)
             logit = (probs * (score_grad - delta)).astype(jnp.bfloat16)
-            w_buf[:span, 2 * t * ROWS:(2 * t + 2) * ROWS] = weights
-            l_buf[:span, 2 * t * ROWS:(2 * t + 2) * ROWS] = logit
+            place = pl.ds(pl.multiple_of(2 * t * ROWS, 2 * ROWS), 2 * ROWS)
+            w_buf[:span, place] = weights
+            l_buf[:span, place] = logit
+            return carry
+
+        lax.fori_loop(0, PER_HEAD // 2, pair_step, 0)
         q_all = jnp.concatenate([q_buf[:, head_cols(t)] for t in range(PER_HEAD)], axis=0)
         grad_all = jnp.concatenate([g_buf[:, head_cols(t)] for t in range(PER_HEAD)], axis=0)
         logit_all = l_buf[:span, :]

time: 36.5 us -> 37.3 us (1.022)
  Pallas kernels: 35.7 us -> 36.5 us
    pallas_call x1, Pallas kernels: 34.5 us -> 35.4 us  [body(): pl.pallas_call(functools.partial(kernel, ctx_size, dp_size), out_shape=(p...]
where the time goes in v4:
time: 37.3 us; the launch traced here: 37.2 us
  Pallas kernels  36.5 us (98%)
  between operations  0.64 us (2%)
    pallas_call x1, Pallas kernels, body(): pl.pallas_call(functools.partial(kernel, ctx_size, dp_size), out_shape=(p...  35.4 us
    pallas_call x1, Pallas kernels, body(): pl.pallas_call(write_out, out_shape=tuple((jax.ShapeDtypeStruct(x.shape,...  1.18 us

profile of v4, /device:TPU:0, one launch (start us, length us, event | category | flops | bytes accessed | tf_op | source)
XLA Modules:
  0.0 37.2 jit_solution(12759133615647656687)
XLA Ops:
  0.6 35.4 %shard_map.101 = (bf16[128,4096]{1,0:T(8,128)(2,1)S(1)}, bf16[128,512]{1,0:T(8,128)(2,1)S(1)}, bf16[128,512]{1,0:T(8,128)(2,1)S(1)}, f32[16,4096]{1,0:T(8,128)S(1)}, f32[16,512]{1,0:T(8,128)S(1)}) custom-call(bf16[128,4096]{1,0:T(8,128)(2,1)} %bitcast.13, bf16[128,512]{1,0:T(8,128)(2,1)} %bitcast.16, bf16[128,512]{1,0:T(8,128)(2,1)} %bitcast.17, ...), custom_call_target="tpu_custom_call" | custom-call | flops 2500000000 | bytes 4000000 | tf_op jit(solution)/shard_map/pallas_call | solution.py:374
  36.0 1.2 %shard_map.102 = (bf16[128,4096]{1,0:T(8,128)(2,1)}, bf16[128,512]{1,0:T(8,128)(2,1)}, bf16[128,512]{1,0:T(8,128)(2,1)}, f32[16,4096]{1,0:T(8,128)}, f32[16,512]{1,0:T(8,128)}) custom-call(bf16[128,4096]{1,0:T(8,128)(2,1)S(1)} %get-tuple-element.15.refs_0_, bf16[128,512]{1,0:T(8,128)(2,1)S(1)} %get-tuple-element.16.refs_1_, ...), custom_call_target="tpu_custom_call" | custom-call | tf_op jit(solution)/shard_map/pallas_call | solution.py:418

commit v5 on v3

--- a/solution.py
+++ b/solution.py
@@ -166,19 +166,20 @@
             device_id_type=MESH,
         )
 
-    def l1_copy(r, origin, target):
-        return pltpu.make_async_remote_copy(
-            src_ref=l1_send.at[target],
-            dst_ref=l1_recv.at[origin],
-            send_sem=l1_ssem.at[r - 1],
-            recv_sem=l1_rsem.at[origin],
+    def l1_copy(n, origin, half, r, target):
+        tiles = pl.ds(3 * half, 2) if n == 0 else pl.ds(2 * half, 3)
+        return pltpu.make_async_remote_copy(
+            src_ref=l1_send.at[target, tiles],
+            dst_ref=l1_recv.at[origin, tiles],
+            send_sem=l1_ssem.at[n, r - 1],
+            recv_sem=l1_rsem.at[n, origin],
             device_id=plane_peer(target),
             device_id_type=MESH,
         )
 
-    def l1_start():
+    def l1_start(n, half):
         for r in range(1, PLANE):
-            l1_copy(r, me, (me + r) % PLANE).start()
+            l1_copy(n, me, half, r, (me + r) % PLANE).start()
 
     def head_step(h, c, blocks):
         span = blocks * ROWS
@@ -230,13 +231,19 @@
         l1_send[2 * kv, VALUE_TILE] = up
         l1_send[2 * kv + 1, VALUE_TILE] = up
         if blocks > 2:
-            pl.when(c == 1)(l1_start)
+            pl.when(c == 1)(functools.partial(l1_start, 1, h))
         dk = (matmul(logit_all, q_all, NN) * SCALE).astype(jnp.bfloat16)
         for b in range(blocks):
             part[h, c, b, 0] = dk[b * ROWS:(b + 1) * ROWS]
             part[h, c, b, 1] = dv[b * ROWS:(b + 1) * ROWS]
-        for b in range(blocks - 1):
-            return_copy(h, c, b, blocks).start()
+        if blocks == 2:
+            return_copy(h, c, 0, blocks).start()
+        elif blocks > 2:
+
+            @pl.when(c == 0)
+            def _():
+                for b in range(blocks - 1):
+                    return_copy(h, c, b, blocks).start()
 
     def stage(h, blocks):
         for b in range(blocks - 1):
@@ -255,6 +262,7 @@
     rank_copy.wait()
     for blocks in (1, 2):
         pl.when(parity == blocks - 1)(functools.partial(stage, first, blocks))
+    l1_start(0, first)
     for copy in query_copies(second):
         copy.wait()
     for blocks in (3, 4):
@@ -263,7 +271,8 @@
     total = l1_send[me].astype(jnp.float32)
     for r in range(1, PLANE):
         e = (me + r) % PLANE
-        l1_copy(r, e, me).wait_recv()
+        l1_copy(0, e, e // 4, r, me).wait_recv()
+        l1_copy(1, e, 1 - e // 4, r, me).wait_recv()
         total = total + l1_recv[e].astype(jnp.float32)
     l2_recv[my_plane] = total.astype(jnp.bfloat16)
 
@@ -279,6 +288,13 @@
 
     for r in range(1, planes):
         l2_copy(r, my_plane, (my_plane + r) % planes).start()
+
+    def last_returns(blocks):
+        for b in range(blocks - 1):
+            return_copy(second, 1, b, blocks).start()
+
+    for blocks in (3, 4):
+        pl.when(parity == blocks - 3)(functools.partial(last_returns, blocks))
 
     def finish(h, place):
         for c in range(2):
@@ -291,9 +307,6 @@
                     acc = acc + arrived[h, c, slot, n].astype(jnp.float32)
                 out[:, cols] = acc.astype(jnp.bfloat16)
 
-    for place in (2, 3):
-        pl.when(parity == place - 2)(functools.partial(finish, second, place))
-
     for r in range(1, planes):
         l2_copy(r, (my_plane + r) % planes, my_plane).wait_recv()
     total = l2_recv[0].astype(jnp.float32)
@@ -313,6 +326,8 @@
 
     for r in range(1, PLANE):
         l3_copy(r, me, (me + r) % PLANE).start()
+    for place in (2, 3):
+        pl.when(parity == place - 2)(functools.partial(finish, second, place))
     for place in (0, 1):
         pl.when(parity == place)(functools.partial(finish, first, place))
     for r in range(1, PLANE):
@@ -342,7 +357,8 @@
     for blocks in (3, 4):
         pl.when(parity == blocks - 3)(functools.partial(returned, second, blocks))
     for r in range(1, PLANE):
-        l1_copy(r, me, (me + r) % PLANE).wait_send()
+        l1_copy(0, me, first, r, (me + r) % PLANE).wait_send()
+        l1_copy(1, me, second, r, (me + r) % PLANE).wait_send()
         l3_copy(r, me, (me + r) % PLANE).wait_send()
     for r in range(1, planes):
         l2_copy(r, my_plane, (my_plane + r) % planes).wait_send()
@@ -397,8 +413,8 @@
             dma((2, PLACES)),
             dma((2, 2, PLACES)),
             dma((2, 2, PLACES - 1)),
-            dma((PLANE - 1,)),
-            dma((PLANE,)),
+            dma((2, PLANE - 1)),
+            dma((2, PLANE)),
             dma((max(planes - 1, 1),)),
             dma((planes,)),
             dma((PLANE - 1,)),

time: 36.5 us -> 36.6 us (level); the launches traced: 36.3 us -> 36.1 us
  no operation moved by 1% of the time
where the time goes in v5:
time: 36.6 us; the launch traced here: 36.1 us
  Pallas kernels  35.4 us (97%)
  between operations  0.64 us (2%)
    pallas_call x1, Pallas kernels, body(): pl.pallas_call(functools.partial(kernel, ctx_size, dp_size), out_shape=(p...  34.2 us
    pallas_call x1, Pallas kernels, body(): pl.pallas_call(write_out, out_shape=tuple((jax.ShapeDtypeStruct(x.shape,...  1.18 us

profile of v5, /device:TPU:0, one launch (start us, length us, event | category | flops | bytes accessed | tf_op | source)
XLA Modules:
  0.0 36.1 jit_solution(14608362417794156157)
XLA Ops:
  0.6 34.2 %shard_map.101 = (bf16[128,4096]{1,0:T(8,128)(2,1)S(1)}, bf16[128,512]{1,0:T(8,128)(2,1)S(1)}, bf16[128,512]{1,0:T(8,128)(2,1)S(1)}, f32[16,4096]{1,0:T(8,128)S(1)}, f32[16,512]{1,0:T(8,128)S(1)}) custom-call(bf16[128,4096]{1,0:T(8,128)(2,1)} %bitcast.13, bf16[128,512]{1,0:T(8,128)(2,1)} %bitcast.16, bf16[128,512]{1,0:T(8,128)(2,1)} %bitcast.17, ...), custom_call_target="tpu_custom_call" | custom-call | flops 2500000000 | bytes 4000000 | tf_op jit(solution)/shard_map/pallas_call | solution.py:386
  34.9 1.2 %shard_map.102 = (bf16[128,4096]{1,0:T(8,128)(2,1)}, bf16[128,512]{1,0:T(8,128)(2,1)}, bf16[128,512]{1,0:T(8,128)(2,1)}, f32[16,4096]{1,0:T(8,128)}, f32[16,512]{1,0:T(8,128)}) custom-call(bf16[128,4096]{1,0:T(8,128)(2,1)S(1)} %get-tuple-element.15.refs_0_, bf16[128,512]{1,0:T(8,128)(2,1)S(1)} %get-tuple-element.16.refs_1_, ...), custom_call_target="tpu_custom_call" | custom-call | tf_op jit(solution)/shard_map/pallas_call | solution.py:430

commit v6 on v3

--- a/solution.py
+++ b/solution.py
@@ -13,7 +13,6 @@
 ROWS = 128
 RANK = 16
 PLACES = 4
-HALF_KEYS = 256
 HALF_QUERIES = 2048
 PLANE = 8
 TILES = 5
@@ -66,13 +65,13 @@
     def other_plane(r):
         return ((r // pairs) * PLACES + g, (r % pairs) * 2 + d % 2)
 
-    def own_copies(h):
+    def own_copies(h, c):
         p = place_of(h)
-        cols = pl.ds(pl.multiple_of(h * HALF_KEYS, HALF_KEYS), HALF_KEYS)
+        cols = pl.ds(pl.multiple_of((2 * h + c) * WIDTH, WIDTH), WIDTH)
         return [
-            pltpu.make_async_copy(k_hbm.at[:, cols], kv_buf.at[h, p, KEY_ROWS], own_sem.at[h, 0]),
-            pltpu.make_async_copy(v_hbm.at[:, cols], kv_buf.at[h, p, VALUE_ROWS], own_sem.at[h, 1]),
-            pltpu.make_async_copy(av_hbm, kv_buf.at[h, p, DOWN_ROWS, pl.ds(0, ROWS)], own_sem.at[h, 2]),
+            pltpu.make_async_copy(k_hbm.at[:, cols], kv_buf.at[h, c, p, KEY_ROWS], own_sem.at[h, c, 0]),
+            pltpu.make_async_copy(v_hbm.at[:, cols], kv_buf.at[h, c, p, VALUE_ROWS], own_sem.at[h, c, 1]),
+            pltpu.make_async_copy(av_hbm, kv_buf.at[h, c, p, DOWN_ROWS], own_sem.at[h, c, 2]),
         ]
 
     def query_copies(h):
@@ -83,9 +82,10 @@
         ]
 
     rank_copy = pltpu.make_async_copy(aq_hbm, aq_buf, load_sem.at[0, 2])
-    for h in (first, second):
-        for copy in own_copies(h):
-            copy.start()
+    for c in range(2):
+        for h in (first, second):
+            for copy in own_copies(h, c):
+                copy.start()
     for copy in query_copies(first):
         copy.start()
     rank_copy.start()
@@ -106,45 +106,46 @@
     greet((beside + 1, d))
     pl.semaphore_wait(barrier, PLANE - 1 + planes - 1 + 2)
 
-    def key_copy(h, p, distance):
-        return pltpu.make_async_remote_copy(
-            src_ref=kv_buf.at[h, p],
-            dst_ref=kv_buf.at[h, p],
-            send_sem=kv_send.at[h, distance - 1],
-            recv_sem=kv_recv.at[h, p],
+    def key_copy(h, c, p, distance):
+        return pltpu.make_async_remote_copy(
+            src_ref=kv_buf.at[h, c, p],
+            dst_ref=kv_buf.at[h, c, p],
+            send_sem=kv_send.at[h, c, distance - 1],
+            recv_sem=kv_recv.at[h, c, p],
             device_id=ahead(distance),
             device_id_type=MESH,
         )
 
-    def key_arrival(h, b):
-        return pltpu.make_async_remote_copy(
-            src_ref=kv_buf.at[h, b],
-            dst_ref=kv_buf.at[h, b],
-            send_sem=kv_send.at[h, 0],
-            recv_sem=kv_recv.at[h, b],
+    def key_arrival(h, c, b):
+        return pltpu.make_async_remote_copy(
+            src_ref=kv_buf.at[h, c, b],
+            dst_ref=kv_buf.at[h, c, b],
+            send_sem=kv_send.at[h, c, 0],
+            recv_sem=kv_recv.at[h, c, b],
             device_id=ahead(1),
             device_id_type=MESH,
         )
 
-    def relay(h):
-        return pltpu.make_async_remote_copy(
-            src_ref=kv_buf.at[h, 0],
-            dst_ref=kv_buf.at[h, 0],
-            send_sem=kv_send.at[h, 2],
-            recv_sem=kv_recv.at[h, 0],
+    def relay(h, c):
+        return pltpu.make_async_remote_copy(
+            src_ref=kv_buf.at[h, c, 0],
+            dst_ref=kv_buf.at[h, c, 0],
+            send_sem=kv_send.at[h, c, 2],
+            recv_sem=kv_recv.at[h, c, 0],
             device_id=ahead(2),
             device_id_type=MESH,
         )
 
-    for copy in own_copies(first) + own_copies(second):
-        copy.wait()
-    for distance in range(1, PLACES - 1):
-        for h in (first, second):
-            p = place_of(h)
-
-            @pl.when(p + distance < PLACES)
-            def _():
-                key_copy(h, p, distance).start()
+    for c in range(2):
+        for copy in own_copies(first, c) + own_copies(second, c):
+            copy.wait()
+        for distance in range(1, PLACES - 1):
+            for h in (first, second):
+                p = place_of(h)
+
+                @pl.when(p + distance < PLACES)
+                def _():
+                    key_copy(h, c, p, distance).start()
 
     def return_copy(h, c, b, blocks):
         return pltpu.make_async_remote_copy(
@@ -182,14 +183,13 @@
 
     def head_step(h, c, blocks):
         span = blocks * ROWS
-        cols = pl.ds(pl.multiple_of(c * WIDTH, WIDTH), WIDTH)
         base = (2 * h + c) * PER_HEAD * WIDTH
 
         def head_cols(t):
             return pl.ds(pl.multiple_of(base + t * WIDTH, WIDTH), WIDTH)
 
-        keys = kv_buf[h, :blocks, KEY_ROWS, cols].reshape(span, WIDTH)
-        vals = kv_buf[h, :blocks, VALUE_ROWS, cols].reshape(span, WIDTH)
+        keys = kv_buf[h, c, :blocks, KEY_ROWS, :].reshape(span, WIDTH)
+        vals = kv_buf[h, c, :blocks, VALUE_ROWS, :].reshape(span, WIDTH)
         key_row = lax.broadcasted_iota(jnp.int32, (ROWS, 2 * ROWS), 0)
         query_col = lax.broadcasted_iota(jnp.int32, (ROWS, 2 * ROWS), 1) % ROWS
         allowed = key_row <= query_col
@@ -224,7 +224,7 @@
         up = matmul(aq_buf[...], dq_out[:, wide], NN).astype(jnp.bfloat16)
         for t in range(PER_HEAD):
             l1_send[t, 3 * h + c] = up[:, t * WIDTH:(t + 1) * WIDTH]
-        value_down = jnp.concatenate([kv_buf[h, b, DOWN_ROWS, :ROWS] for b in range(blocks)], axis=1)
+        value_down = jnp.concatenate([kv_buf[h, c, b, DOWN_ROWS, :] for b in range(blocks)], axis=1)
         up = matmul(value_down, dv, NN).astype(jnp.bfloat16)
         kv = 2 * h + c
         l1_send[2 * kv, VALUE_TILE] = up
@@ -239,12 +239,11 @@
             return_copy(h, c, b, blocks).start()
 
     def stage(h, blocks):
-        for b in range(blocks - 1):
-            key_arrival(h, b).wait_recv()
-        if blocks == 2:
-            relay(h).start()
-
         def one(c, carry):
+            for b in range(blocks - 1):
+                key_arrival(h, c, b).wait_recv()
+            if blocks == 2:
+                relay(h, c).start()
             head_step(h, c, blocks)
             return carry
 
@@ -324,14 +323,19 @@
     for kv in range(KEY_VALUE_HEADS):
         uv_out[:, kv * WIDTH:(kv + 1) * WIDTH] = l3_recv[2 * kv, VALUE_TILE].astype(jnp.float32)
 
-    pl.when(parity == 1)(lambda: relay(first).wait_send())
+    @pl.when(parity == 1)
+    def _():
+        for c in range(2):
+            relay(first, c).wait_send()
+
     for h in (first, second):
         p = place_of(h)
         for distance in range(1, PLACES - 1):
 
             @pl.when(p + distance < PLACES)
             def _():
-                key_copy(h, p, distance).wait_send()
+                for c in range(2):
+                    key_copy(h, c, p, distance).wait_send()
 
     def returned(h, blocks):
         for c in range(2):
@@ -382,7 +386,7 @@
             pltpu.VMEM((ROWS, KEY_VALUE_HEADS * wide), bf16),
             pltpu.VMEM((ROWS, KEY_VALUE_HEADS * wide), bf16),
             pltpu.VMEM((RANK, ROWS), bf16),
-            pltpu.VMEM((2, PLACES, 2 * ROWS + RANK, HALF_KEYS), bf16),
+            pltpu.VMEM((2, 2, PLACES, 2 * ROWS + RANK, WIDTH), bf16),
             pltpu.VMEM((PLACES * ROWS, wide), bf16),
             pltpu.VMEM((PLACES * ROWS, wide), bf16),
             pltpu.VMEM((2, 2, PLACES, 2, ROWS, WIDTH), bf16),
@@ -392,9 +396,9 @@
             pltpu.VMEM((planes, TILES, RANK, WIDTH), bf16),
             pltpu.VMEM((PLANE, TILES, RANK, WIDTH), bf16),
             dma((2, 3)),
-            dma((2, 3)),
-            dma((2, PLACES - 1)),
-            dma((2, PLACES)),
+            dma((2, 2, 3)),
+            dma((2, 2, PLACES - 1)),
+            dma((2, 2, PLACES)),
             dma((2, 2, PLACES)),
             dma((2, 2, PLACES - 1)),
             dma((PLANE - 1,)),

time: 36.5 us -> 35.8 us (0.981)
  Pallas kernels: 35.7 us -> 35 us
    pallas_call x1, Pallas kernels: 34.5 us -> 33.8 us  [body(): pl.pallas_call(functools.partial(kernel, ctx_size, dp_size), out_shape=(p...]
where the time goes in v6:
time: 35.8 us; the launch traced here: 35.6 us
  Pallas kernels  35 us (98%)
  between operations  0.64 us (2%)
    pallas_call x1, Pallas kernels, body(): pl.pallas_call(functools.partial(kernel, ctx_size, dp_size), out_shape=(p...  33.8 us
    pallas_call x1, Pallas kernels, body(): pl.pallas_call(write_out, out_shape=tuple((jax.ShapeDtypeStruct(x.shape,...  1.18 us

profile of v6, /device:TPU:0, one launch (start us, length us, event | category | flops | bytes accessed | tf_op | source)
XLA Modules:
  0.0 35.6 jit_solution(6717780623453046699)
XLA Ops:
  0.6 33.8 %shard_map.101 = (bf16[128,4096]{1,0:T(8,128)(2,1)S(1)}, bf16[128,512]{1,0:T(8,128)(2,1)S(1)}, bf16[128,512]{1,0:T(8,128)(2,1)S(1)}, f32[16,4096]{1,0:T(8,128)S(1)}, f32[16,512]{1,0:T(8,128)S(1)}) custom-call(bf16[128,4096]{1,0:T(8,128)(2,1)} %bitcast.13, bf16[128,512]{1,0:T(8,128)(2,1)} %bitcast.16, bf16[128,512]{1,0:T(8,128)(2,1)} %bitcast.17, ...), custom_call_target="tpu_custom_call" | custom-call | flops 2500000000 | bytes 4000000 | tf_op jit(solution)/shard_map/pallas_call | solution.py:374
  34.5 1.2 %shard_map.102 = (bf16[128,4096]{1,0:T(8,128)(2,1)}, bf16[128,512]{1,0:T(8,128)(2,1)}, bf16[128,512]{1,0:T(8,128)(2,1)}, f32[16,4096]{1,0:T(8,128)}, f32[16,512]{1,0:T(8,128)}) custom-call(bf16[128,4096]{1,0:T(8,128)(2,1)S(1)} %get-tuple-element.15.refs_0_, bf16[128,512]{1,0:T(8,128)(2,1)S(1)} %get-tuple-element.16.refs_1_, ...), custom_call_target="tpu_custom_call" | custom-call | tf_op jit(solution)/shard_map/pallas_call | solution.py:418
